TPU v7x, 128 devices: a whole 4x4x4 slice. The times are simulated.
128 devices in a mesh: row: 16 (over x, z), grp: 8 (over y, core).
Axes of the slice: x: 4, y: 4, z: 4, core: 2. Of those that a mesh axis runs over, the one named last changes fastest.
Arguments:
- sketch: bfloat16 [1024, 256, 256], P(('row', 'grp')), may hold values from -6 to 6
- band_tiles: bfloat16 [1024, 3, 256, 256], P(('row', 'grp')), may hold values from -0.125 to 0.125
- far_tiles: bfloat16 [1024, 8, 256, 256], P(('row', 'grp')), may hold values from -0.125 to 0.125
- far_owner: int32 [1024, 8], P(('row', 'grp')), may hold values from 0 to 15, all different within a row; in each aligned block of 8 rows (0 to 7, 8 to 15, ...) at most 6 rows name the same one
- far_local: int32 [1024, 8], P(('row', 'grp')), may hold values from 0 to 7
- far_count: int32 [1024], P(('row', 'grp')), may hold values from 1 to 8, as said below
Outputs:
- basis: float32 [1024, 256, 256], P(('row', 'grp'))
- factor: float32 [256, 256], replicated
Inputs may be any that keep to these rules, and one draw needn't show every extreme that they name: `far_owner`: in the 8 block rows of one device, the entries of one row are distinct, and no value is named by more than 6 entries; some value reaches 6. `far_count`: the first block row of every device has 8 live slots.
All inputs are finite; a program needn't handle non-finite values.
Results may differ from a plain program's by a relative error of at most 0.003.
Values may be sent and summed in bfloat16 or wider, within the bound.
A program may use at most 128 MiB of HBM per device.

v0:
```python
import math

import jax
import jax.numpy as jnp
from jax import lax
from jax.sharding import PartitionSpec as P


def with_halo(cells, sides, width):
    for axis, dim in sides:
        count = lax.axis_size(axis)
        ends = count - 1
        head = lax.slice_in_dim(cells, 0, width, axis=dim)
        tail = lax.slice_in_dim(cells, cells.shape[dim] - width, cells.shape[dim], axis=dim)
        cells = jnp.concatenate(
            [
                lax.ppermute(tail, axis, [(i, (i + 1) % count) for i in range(ends)]),
                cells,
                lax.ppermute(head, axis, [((i + 1) % count, i) for i in range(ends)]),
            ],
            axis=dim,
        )
    return cells


def body(sketch, band_tiles, far_tiles, far_owner, far_local, far_count):
    row_count = lax.axis_size("row")
    blocks = sketch.shape[0]
    width = sketch.shape[1]
    columns_k = sketch.shape[2]
    slots = far_tiles.shape[1]
    capacity = min(blocks, blocks * slots // row_count + 2)
    owner = far_owner.reshape(-1)
    local_index = far_local.reshape(-1)
    owner_hot = (owner[:, None] == jnp.arange(row_count, dtype=jnp.int32)[None, :]).astype(
        jnp.int32
    )
    slot_rank = jnp.sum((jnp.cumsum(owner_hot, axis=0) - 1) * owner_hot, axis=1)
    slot_index = owner * capacity + slot_rank
    positions = jnp.arange(row_count * capacity, dtype=jnp.int32)
    requests = jnp.sum(
        jnp.where(slot_index[:, None] == positions[None, :], local_index[:, None], 0), axis=0
    )
    requests = requests.reshape(row_count, capacity)
    live_mask = (jnp.arange(slots, dtype=jnp.int32)[None, :] < far_count[:, None]).astype(
        jnp.bfloat16
    )

    def fetch_blocks(panel):
        tile_stack = panel[lax.all_to_all(requests, "row", split_axis=0, concat_axis=0, tiled=True)]
        arrived = lax.all_to_all(tile_stack, "row", split_axis=0, concat_axis=0, tiled=True)
        return arrived.reshape(row_count * capacity, width, columns_k)[slot_index]

    def apply_matrix(panel):
        padded = with_halo(panel, ((("row", "grp"), 0),), 1)
        result = jnp.zeros((blocks, width, columns_k), jnp.float32)
        for offset in range(3):
            result = result + jnp.einsum(
                "iab,ibk->iak",
                band_tiles[:, offset],
                padded[offset : offset + blocks],
                preferred_element_type=jnp.float32,
            )
        remote = (
            fetch_blocks(panel).reshape(blocks, slots, width, columns_k)
            * live_mask[:, :, None, None]
        )
        result = result + jnp.einsum(
            "isab,isbk->iak", far_tiles, remote, preferred_element_type=jnp.float32
        )
        return result

    first = apply_matrix(sketch).astype(jnp.bfloat16)
    second = apply_matrix(first)
    flat_rows = second.reshape(blocks * width, columns_k)
    gram_part = jnp.dot(
        flat_rows.T, flat_rows, precision=lax.Precision.HIGHEST, preferred_element_type=jnp.float32
    )
    gram = lax.psum(gram_part, ("row", "grp"))
    lower_factor = jnp.linalg.cholesky(gram)
    solved = jax.scipy.linalg.solve_triangular(lower_factor, flat_rows.T, lower=True)
    scale_rows = math.sqrt(blocks * width * lax.axis_size("row") * lax.axis_size("grp"))
    basis = (solved.T * scale_rows).reshape(blocks, width, columns_k)
    factor = lower_factor.T / scale_rows
    return (basis, factor)


def solution(mesh):
    in_specs = (
        P(("row", "grp"), None, None),
        P(("row", "grp"), None, None, None),
        P(("row", "grp"), None, None, None),
        P(("row", "grp"), None),
        P(("row", "grp"), None),
        P(("row", "grp")),
    )
    out_specs = (P(("row", "grp"), None, None), P())
    return jax.shard_map(body, mesh=mesh, in_specs=in_specs, out_specs=out_specs, check_vma=False)
```

profile of v0, /device:TPU:1, one launch (start us, length us, event | category | flops | bytes accessed | tf_op | source)
XLA Modules:
  0.0 753.5 jit_solution(13790640195730076622)
XLA Ops:
  9.3 14.6 %all_to_all.23 = s32[16,1,6]{2,1,0:T(1,128)S(1)} all-to-all(s32[16,1,6]{2,1,0:T(1,128)S(1)} %bitcast.115), channel_id=1, replica_groups=mesh['row'=16,'grp'=8] {'row'}, dimensions={0} | all-to-all | bytes 768 | tf_op jit(solution)/shard_map/all_to_all | solution.py:50
  24.2 7.9 %gather_fusion = bf16[96,256,256]{2,1,0:T(8,128)(2,1)} fusion(bf16[8,256,256]{2,1,0:T(8,128)(2,1)} %param.6, s32[1024]{0:T(1024)S(1)} %pad_clamp_fusion.1), kind=kCustom, calls=%fused_computation | custom fusion | bytes 25166208 | tf_op jit(solution)/shard_map/gather | solution.py:50
  32.1 5.1 all-to-all-start.1
  37.7 5.2 collective-permute-start
  43.0 1.9 collective-permute-start.1
  45.1 1.8 fusion.36
  46.9 3.1 fusion.10
  50.1 203.0 %all-to-all-done.1 = bf16[16,6,256,256]{3,2,1,0:T(8,128)(2,1)} async-done(((bf16[16,6,256,256]{3,2,1,0:T(8,128)(2,1)}), bf16[16,6,256,256]{3,2,1,0:T(8,128)(2,1)}, u32[]{:S(2)}, u32[]{:S(2)}) %all-to-all-start.1) | async-done | bytes 12582944 | tf_op jit(solution)/shard_map/all_to_all | solution.py:51
  253.1 10.1 %gather_fusion.1 = bf16[64,256,256]{2,1,0:T(8,128)(2,1)} fusion(bf16[96,256,256]{2,1,0:T(8,128)(2,1)} %bitcast.8, s32[1024]{0:T(1024)S(1)} %pad_clamp_fusion), kind=kCustom, calls=%fused_computation.1 | custom fusion | bytes 16777472 | tf_op jit(solution)/shard_map/gather | solution.py:52
  263.2 9.9 %fusion.2 = f32[8,256,256,1]{2,1,3,0:T(8,128)} fusion(bf16[8,8,256,256]{3,2,1,0:T(8,128)(2,1)} %param.8, bf16[8,8,256,256]{3,2,1,0:T(8,128)(2,1)} %bitcast.110, bf16[8,8]{1,0:T(8,128)(2,1)S(1)} %fusion.54), kind=kOutput, calls=%fused_computation.8 | convolution fusion | flops 2151677952 | bytes 18874496 | tf_op jit(solution)/shard_map/isab,isbk->iak/dot_general | solution.py:68
  273.1 3.4 fusion.7
  276.4 6.7 gather_fusion.2
  283.1 10.5 %all-to-all-start.2 = ((bf16[16,6,256,256]{2,3,1,0:T(8,128)(2,1)}), bf16[16,6,256,256]{2,3,1,0:T(8,128)(2,1)}, u32[]{:S(2)}, u32[]{:S(2)}) async-start(bf16[16,6,256,256]{2,3,1,0:T(8,128)(2,1)} %bitcast.107), calls=%async_computation.2 | async-start | bytes 25165824 | tf_op jit(solution)/shard_map/all_to_all | solution.py:51
  293.7 7.0 collective-permute-start.2
  300.7 3.1 fusion.34
  303.7 2.1 collective-permute-start.3
  305.8 3.0 fusion.17
  308.8 178.3 %all-to-all-done.2 = bf16[16,6,256,256]{2,3,1,0:T(8,128)(2,1)} async-done(((bf16[16,6,256,256]{2,3,1,0:T(8,128)(2,1)}), bf16[16,6,256,256]{2,3,1,0:T(8,128)(2,1)}, u32[]{:S(2)}, u32[]{:S(2)}) %all-to-all-start.2) | async-done | bytes 12582944 | tf_op jit(solution)/shard_map/all_to_all | solution.py:51
  487.1 16.7 %copy.84 = bf16[16,6,256,256]{3,2,1,0:T(8,128)(2,1)} copy(bf16[16,6,256,256]{2,3,1,0:T(8,128)(2,1)} %all-to-all-done.2) | data formatting | bytes 25165824 | tf_op jit(solution)/shard_map/all_to_all | solution.py:51
  503.8 10.1 %gather_fusion.3 = bf16[64,256,256]{2,1,0:T(8,128)(2,1)} fusion(bf16[96,256,256]{2,1,0:T(8,128)(2,1)} %bitcast.108, s32[1024]{0:T(1024)S(1)} %pad_clamp_fusion), kind=kCustom, calls=%fused_computation.3 | custom fusion | bytes 16777472 | tf_op jit(solution)/shard_map/gather | solution.py:52
  513.9 8.4 %fusion = f32[8,256,256,1]{1,2,3,0:T(8,128)S(1)} fusion(bf16[8,8,256,256]{3,2,1,0:T(8,128)(2,1)} %param.8, bf16[8,8,256,256]{3,2,1,0:T(8,128)(2,1)} %bitcast.109, bf16[8,8]{1,0:T(8,128)(2,1)S(1)} %fusion.54), kind=kOutput, calls=%fused_computation.6 | convolution fusion | flops 2164260864 | bytes 18874496 | tf_op jit(solution)/shard_map/isab,isbk->iak/dot_general | solution.py:68
  522.3 1.9 bitcast_add_fusion.1
  524.2 4.2 fusion.27
  528.4 2.1 copy.88
  530.5 148.3 %all-reduce.3.cloned.1.call-done = f32[256,256]{0,1:T(8,128)} async-done(((f32[256,256]{0,1:T(8,128)}), f32[256,256]{0,1:T(8,128)}) %all-reduce.3.cloned.1.call-update) | async-done | bytes 262160 | tf_op jit(solution)/shard_map/psum | solution.py:79
  680.9 11.7 %cholesky.50 = f32[128,128]{1,0:T(8,128)S(1)} custom-call(f32[128,128]{1,0:T(8,128)S(1)} %cholesky.118), custom_call_target="Cholesky" | custom-call | tf_op jit(solution)/shard_map/jit(cholesky)/cholesky | solution.py:80
  692.7 9.8 %custom-call.15 = f32[1,128,128]{1,2,0:T(8,128)S(1)} custom-call(f32[1,128,128]{2,1,0:T(8,128)S(1)} %get-tuple-element.37), custom_call_target="InvertDiagBlocksLowerTriangular" | custom-call | tf_op jit(solution)/shard_map/jit(cholesky)/cholesky | solution.py:80
  703.0 11.7 %cholesky.105 = f32[128,128]{1,0:T(8,128)S(1)} custom-call(f32[128,128]{1,0:T(8,128)S(1)} %convolution_subtract_fusion.1), custom_call_target="Cholesky" | custom-call | tf_op jit(solution)/shard_map/jit(cholesky)/cholesky | solution.py:80
  716.8 4.0 while.1
  717.4 1.4 bitcast_dynamic-update-slice_fusion.2
  720.8 19.9 %custom-call.16 = f32[2,128,128]{1,2,0:T(8,128)S(1)} custom-call(f32[2,128,128]{2,1,0:T(8,128)S(1)} %get-tuple-element.9), custom_call_target="InvertDiagBlocksLowerTriangular" | custom-call | tf_op jit(solution)/shard_map/jit(_solve_triangular)/triangular_solve | solution.py:81
  744.0 1.8 copy.101
  (66 shorter events, 13.2 us)
Async XLA Ops:
  32.1 5.1 copy-start
  32.1 221.0 %all-to-all-start.1 = ((bf16[16,6,256,256]{3,2,1,0:T(8,128)(2,1)}), bf16[16,6,256,256]{3,2,1,0:T(8,128)(2,1)}, u32[]{:S(2)}, u32[]{:S(2)}) async-start(bf16[16,6,256,256]{3,2,1,0:T(8,128)(2,1)} %bitcast.106), calls=%async_computation.1 | async-start | bytes 25165824 | tf_op jit(solution)/shard_map/all_to_all | solution.py:51
  37.2 7.7 %copy-start.5 = (s32[8,8]{1,0:T(8,128)S(1)}, s32[8,8]{1,0:T(8,128)}, u32[]{:S(2)}) copy-start(s32[8,8]{1,0:T(8,128)} %param.9) | copy-start | bytes 772
  37.2 7.8 %copy-start.6 = (s32[8]{0:T(128)S(1)}, s32[8]{0:T(128)}, u32[]{:S(2)}) copy-start(s32[8]{0:T(128)} %param.11) | copy-start | bytes 100
  37.7 7.3 copy-start.3
  37.7 9.2 %collective-permute-start = (bf16[1,256,256]{1,2,0:T(8,128)(2,1)S(1)}, bf16[1,256,256]{1,2,0:T(8,128)(2,1)}, u32[]{:S(2)}, u32[]{:S(2)}) collective-permute-start(bf16[1,256,256]{1,2,0:T(8,128)(2,1)S(1)} %get-tuple-element.31), channel_id=1, source_target_pairs={{0,1},{1,2},{2,3},{3,4},{4,5},{5,6},{6,7},{7,8},{8,9},{9,10},{10,1... | collective-permute-start | bytes 393224 | tf_op jit(solution)/shard_map/ppermute | solution.py:17
  43.0 230.1 %collective-permute-start.1 = (bf16[1,256,256]{1,2,0:T(8,128)(2,1)S(1)}, bf16[1,256,256]{1,2,0:T(8,128)(2,1)S(1)}, u32[]{:S(2)}, u32[]{:S(2)}) collective-permute-start(bf16[1,256,256]{1,2,0:T(8,128)(2,1)S(1)} %get-tuple-element.30), channel_id=1, source_target_pairs={{1,0},{2,1},{3,2},{4,3},{5,4},{6,5},{7,6},{8,7},{9,8},{10,9},{11,1... | collective-permute-start | bytes 393224 | tf_op jit(solution)/shard_map/ppermute | solution.py:19
  45.1 1.9 copy-start.4
  283.1 204.0 %all-to-all-start.2 = ((bf16[16,6,256,256]{2,3,1,0:T(8,128)(2,1)}), bf16[16,6,256,256]{2,3,1,0:T(8,128)(2,1)}, u32[]{:S(2)}, u32[]{:S(2)}) async-start(bf16[16,6,256,256]{2,3,1,0:T(8,128)(2,1)} %bitcast.107), calls=%async_computation.2 | async-start | bytes 25165824 | tf_op jit(solution)/shard_map/all_to_all | solution.py:51
  293.6 385.2 %all-reduce.3.cloned.1.call-start = ((), (), s32[]{:S(2)}) async-start(), calls=%async_computation.3 | async-start | bytes 524288 | tf_op jit(solution)/shard_map/psum | solution.py:79
  293.7 12.2 %collective-permute-start.2 = (bf16[1,256,256]{1,2,0:T(8,128)(2,1)S(1)}, bf16[1,256,256]{1,2,0:T(8,128)(2,1)S(1)}, u32[]{:S(2)}, u32[]{:S(2)}) collective-permute-start(bf16[1,256,256]{1,2,0:T(8,128)(2,1)S(1)} %get-tuple-element.29), channel_id=1, source_target_pairs={{0,1},{1,2},{2,3},{3,4},{4,5},{5,6},{6,7},{7,8},{8,9},{9,10},{10,1... | collective-permute-start | bytes 393224 | tf_op jit(solution)/shard_map/ppermute | solution.py:17
  303.7 218.5 %collective-permute-start.3 = (bf16[1,256,256]{1,2,0:T(8,128)(2,1)S(1)}, bf16[1,256,256]{1,2,0:T(8,128)(2,1)S(1)}, u32[]{:S(2)}, u32[]{:S(2)}) collective-permute-start(bf16[1,256,256]{1,2,0:T(8,128)(2,1)S(1)} %get-tuple-element.28), channel_id=1, source_target_pairs={{1,0},{2,1},{3,2},{4,3},{5,4},{6,5},{7,6},{8,7},{9,8},{10,9},{11,1... | collective-permute-start | bytes 393224 | tf_op jit(solution)/shard_map/ppermute | solution.py:19
  513.9 8.4 %copy-start.2 = (f32[8,256,256]{1,2,0:T(8,128)S(1)}, f32[8,256,256]{1,2,0:T(8,128)}, u32[]{:S(2)}) copy-start(f32[8,256,256]{1,2,0:T(8,128)} %fusion.34) | copy-start | bytes 6291460
  513.9 8.4 %copy-start.7 = (f32[8,256,256]{1,2,0:T(8,128)S(1)}, f32[8,256,256]{1,2,0:T(8,128)}, u32[]{:S(2)}) copy-start(f32[8,256,256]{1,2,0:T(8,128)} %fusion.17) | copy-start | bytes 6291460
  524.2 4.2 copy-start.1
Sparse Core Ops, SparseCore 0:
  528.5 150.2 all-reduce.2
where the time goes:
time: 755 us; the launch traced here: 753 us
  waiting for transfers between devices  530 us (70%)
  local copies, waits for them, and re-layouts  63.9 us (8%)
  other arithmetic  55.6 us (7%)
  matrix products  42.2 us (6%)
  starting transfers between devices  31.8 us (4%)
  between operations  15.7 us (2%)
  blocking collectives  14.6 us (2%)
    all_to_all x2, waiting for transfers between devices, fetch_blocks(): lax.all_to_all(tile_stack, 'row', split_axis=0, concat_axis=0, tiled=True)  381 us
    psum x1, waiting for transfers between devices, body(): gram = lax.psum(gram_part, ('row', 'grp'))  148 us
    another operation x6, other arithmetic, body(): lower_factor = jnp.linalg.cholesky(gram)  33.9 us
    gather x2, local copies, waits for them, and re-layouts, fetch_blocks(): return arrived.reshape(row_count * capacity, width, columns_k)[slot_index]  20.2 us
    another operation x2, other arithmetic, body(): jax.scipy.linalg.solve_triangular(lower_factor, flat_rows.T, lower=True)  19.9 us
    dot_general x2, matrix products, apply_matrix(): jnp.einsum('isab,isbk->iak', far_tiles, remote, preferred_element_type=jn...  18.2 us
    all_to_all x1, local copies, waits for them, and re-layouts, fetch_blocks(): lax.all_to_all(tile_stack, 'row', split_axis=0, concat_axis=0, tiled=True)  16.7 us
    dot_general x6, matrix products, apply_matrix(): jnp.einsum('iab,ibk->iak', band_tiles[:, offset], padded[offset:offset +...  16.3 us
  transfers between devices with their start and end apart: 7, of which 3 were waited for; matrix products, arithmetic and copies ran while one was open for 9% of the time, Pallas kernels for 0%

commit v1 on v0

v1 whole, which is shorter than its diff:
```python
import functools
import math

import jax
import jax.numpy as jnp
from jax import lax
from jax.experimental import pallas as pl
from jax.experimental.pallas import tpu as pltpu
from jax.sharding import PartitionSpec as P

MESH = pl.DeviceIdType.MESH
SIDE = 4
N_ROW = SIDE * SIDE
N_GRP = 8
BLOCKS = 8
SLOTS = 8
B = 256
N_PANEL = N_ROW * BLOCKS
ZERO, LEFT, RIGHT = N_PANEL, N_PANEL + 1, N_PANEL + 2
PART = B // N_ROW
F32 = jnp.float32
BF16 = jnp.bfloat16


def dot(a, b):
    return jnp.dot(a, b, preferred_element_type=F32)


def range_kernel(
    sketch, band, far, owner, local, count,
    second_out, gram_out,
    panel_a, panel_b, band_v, far_v, acc, gram_v, gram_c, parts, shares,
    load_sem, recv_sem, send_sem, halo_send, halo_recv,
    scatter_send, scatter_recv, share_send, share_recv, spread_send, spread_recv, out_sem,
):
    row, grp = lax.axis_index("row"), lax.axis_index("grp")
    x, z = row // SIDE, row % SIDE
    device = row * N_GRP + grp
    after, before = (device + 1) % (N_ROW * N_GRP), (device + N_ROW * N_GRP - 1) % (N_ROW * N_GRP)
    after_id = (after // N_GRP, after % N_GRP)
    before_id = (before // N_GRP, before % N_GRP)
    own = row * BLOCKS

    load_panel = pltpu.make_async_copy(sketch, panel_a.at[pl.ds(own, BLOCKS)], load_sem.at[0])
    load_band = pltpu.make_async_copy(band, band_v, load_sem.at[1])
    load_far = pltpu.make_async_copy(far, far_v, load_sem.at[2])
    load_panel.start()
    load_band.start()
    load_far.start()

    barrier = pltpu.get_barrier_semaphore()

    def greet(device_id):
        pl.semaphore_signal(barrier, inc=1, device_id=device_id, device_id_type=MESH)

    @pl.loop(1, N_ROW)
    def _(k):
        greet(((row + k) % N_ROW, grp))

    @pl.loop(1, N_GRP)
    def _(k):
        greet((row, (grp + k) % N_GRP))

    greet(after_id)
    greet(before_id)
    for panel in (panel_a, panel_b):
        panel[ZERO] = jnp.zeros((B, B), BF16)
    load_panel.wait()
    pl.semaphore_wait(barrier, N_ROW - 1 + N_GRP - 1 + 2)

    def gather_steps(app, panel):
        def place(b, first, second):
            swap = b % 2
            sign = 1 - 2 * ((b // 2) % 2)
            to_x = (x + 2 * SIDE + sign * (first * (1 - swap) + second * swap)) % SIDE
            to_z = (z + 2 * SIDE + sign * (first * swap + second * (1 - swap))) % SIDE
            return to_x * SIDE + to_z

        def send(b, u, v, first, second):
            slot = place(b, -u, -v) * BLOCKS + b
            to_u, to_v = (u + first) % SIDE, (v + second) % SIDE
            pltpu.make_async_remote_copy(
                src_ref=panel.at[slot],
                dst_ref=panel.at[slot],
                send_sem=send_sem.at[app, b],
                recv_sem=recv_sem.at[app, b, to_u * SIDE + to_v],
                device_id=(place(b, first, second), grp),
                device_id_type=MESH,
            ).start()

        def arrived(b, u, v):
            slot = place(b, -u, -v) * BLOCKS + b
            pltpu.make_async_copy(
                panel.at[slot], panel.at[slot], recv_sem.at[app, b, u * SIDE + v]
            ).wait()

        def send_own(b):
            send(b, 0, 0, 1, 0)
            send(b, 0, 0, -1, 0)
            send(b, 0, 0, 0, 1)
            send(b, 0, 0, 0, -1)

        def forward():
            @pl.loop(0, BLOCKS)
            def _(b):
                arrived(b, 1, 0)
                send(b, 1, 0, 1, 0)
                send(b, 1, 0, 0, 1)
                send(b, 1, 0, 0, -1)
                arrived(b, 3, 0)
                send(b, 3, 0, 0, 1)
                send(b, 3, 0, 0, -1)

            @pl.loop(0, BLOCKS)
            def _(b):
                arrived(b, 2, 0)
                send(b, 2, 0, 0, 1)
                send(b, 2, 0, 0, -1)
                arrived(b, 0, 1)
                send(b, 0, 1, 0, 1)

            @pl.loop(0, BLOCKS)
            def _(b):
                arrived(b, 1, 1)
                send(b, 1, 1, 0, 1)
                arrived(b, 3, 1)
                send(b, 3, 1, 0, 1)

            @pl.loop(0, BLOCKS)
            def _(b):
                arrived(b, 2, 1)
                send(b, 2, 1, 0, 1)

            @pl.loop(0, BLOCKS)
            def _(b):
                for u in range(SIDE):
                    arrived(b, u, 3)
                for u in range(SIDE):
                    arrived(b, u, 2)

        def sent():
            @pl.loop(0, BLOCKS)
            def _(b):
                pltpu.make_async_copy(
                    panel.at[pl.ds(0, N_ROW - 1)],
                    panel.at[pl.ds(0, N_ROW - 1)],
                    send_sem.at[app, b],
                ).wait()

        return send_own, forward, sent

    def halo(app, panel):
        tail = pltpu.make_async_remote_copy(
            src_ref=panel.at[own + BLOCKS - 1],
            dst_ref=panel.at[LEFT],
            send_sem=halo_send.at[app, 0],
            recv_sem=halo_recv.at[app, 0],
            device_id=after_id,
            device_id_type=MESH,
        )
        head = pltpu.make_async_remote_copy(
            src_ref=panel.at[own],
            dst_ref=panel.at[RIGHT],
            send_sem=halo_send.at[app, 1],
            recv_sem=halo_recv.at[app, 1],
            device_id=before_id,
            device_id_type=MESH,
        )
        return head, tail

    def near(panel, i):
        left = jnp.where(i == 0, jnp.where(device == 0, ZERO, LEFT), own + i - 1)
        right = jnp.where(
            i == BLOCKS - 1,
            jnp.where(device == N_ROW * N_GRP - 1, ZERO, RIGHT),
            own + i + 1,
        )
        return (
            dot(band_v[i, 0], panel[left])
            + dot(band_v[i, 1], panel[own + i])
            + dot(band_v[i, 2], panel[right])
        )

    def long_range(panel, i):
        total = acc[i]
        live_slots = count[i]
        for s in range(SLOTS):
            live = (s < live_slots).astype(jnp.int32)
            index = (owner[i, s] * BLOCKS + local[i, s]) * live + ZERO * (1 - live)
            total = total + dot(far_v[i, s], panel[index])
        return total

    send_own, forward, sent_a = gather_steps(0, panel_a)
    head, tail = halo(0, panel_a)
    pl.loop(0, BLOCKS)(send_own)
    head.start()
    tail.start()
    load_band.wait()
    head.wait()
    tail.wait()

    @pl.loop(0, BLOCKS)
    def _(i):
        acc[i] = near(panel_a, i)

    forward()
    load_far.wait()

    send_own, forward, sent_b = gather_steps(1, panel_b)
    head, tail = halo(1, panel_b)

    @pl.loop(0, BLOCKS)
    def _(i):
        panel_b[own + i] = long_range(panel_a, i).astype(BF16)
        send_own(i)

    head.start()
    tail.start()
    head.wait()
    tail.wait()

    @pl.loop(0, BLOCKS)
    def _(i):
        acc[i] = near(panel_b, i)

    forward()

    gram_v[...] = jnp.zeros((B, B), F32)
    gram_c[...] = jnp.zeros((B, B), F32)

    @pl.loop(0, BLOCKS)
    def _(i):
        block = long_range(panel_b, i)
        acc[i] = block
        top = block.astype(BF16)
        rest = block - top.astype(F32)
        middle = rest.astype(BF16)
        low = (rest - middle.astype(F32)).astype(BF16)
        top_t = top.T
        gram_v[...] += dot(top_t, top) + dot(middle.T, middle)
        gram_c[...] += dot(top_t, middle) + dot(top_t, low)

    store = pltpu.make_async_copy(acc, second_out, out_sem.at[0])
    store.start()
    cross = gram_c[...]
    gram_v[...] += cross + cross.T

    def scatter(k):
        to = (row + k) % N_ROW
        return pltpu.make_async_remote_copy(
            src_ref=gram_v.at[pl.ds(to * PART, PART)],
            dst_ref=parts.at[row],
            send_sem=scatter_send.at[k],
            recv_sem=scatter_recv.at[k],
            device_id=(to, grp),
            device_id_type=MESH,
        )

    @pl.loop(1, N_ROW)
    def _(k):
        scatter(k).start()

    parts[row] = gram_v[pl.ds(row * PART, PART)]

    @pl.loop(1, N_ROW)
    def _(k):
        origin = (row + N_ROW - k) % N_ROW
        pltpu.make_async_copy(parts.at[origin], parts.at[origin], scatter_recv.at[k]).wait()

    total = parts[0]
    for k in range(1, N_ROW):
        total = total + parts[k]
    shares[grp] = total

    def share(k):
        return pltpu.make_async_remote_copy(
            src_ref=shares.at[grp],
            dst_ref=shares.at[grp],
            send_sem=share_send.at[k],
            recv_sem=share_recv.at[k],
            device_id=(row, (grp + k) % N_GRP),
            device_id_type=MESH,
        )

    @pl.loop(1, N_GRP)
    def _(k):
        share(k).start()

    @pl.loop(1, N_GRP)
    def _(k):
        origin = (grp + N_GRP - k) % N_GRP
        pltpu.make_async_copy(shares.at[origin], shares.at[origin], share_recv.at[k]).wait()

    total = shares[0]
    for k in range(1, N_GRP):
        total = total + shares[k]
    gram_c[pl.ds(row * PART, PART)] = total

    def spread(k):
        mine = pl.ds(row * PART, PART)
        return pltpu.make_async_remote_copy(
            src_ref=gram_c.at[mine],
            dst_ref=gram_c.at[mine],
            send_sem=spread_send.at[k],
            recv_sem=spread_recv.at[k],
            device_id=((row + k) % N_ROW, grp),
            device_id_type=MESH,
        )

    @pl.loop(1, N_ROW)
    def _(k):
        spread(k).start()

    @pl.loop(1, N_ROW)
    def _(k):
        theirs = pl.ds(((row + N_ROW - k) % N_ROW) * PART, PART)
        pltpu.make_async_copy(gram_c.at[theirs], gram_c.at[theirs], spread_recv.at[k]).wait()

    @pl.loop(1, N_ROW)
    def _(k):
        scatter(k).wait_send()
        spread(k).wait_send()

    @pl.loop(1, N_GRP)
    def _(k):
        share(k).wait_send()

    finish = pltpu.make_async_copy(gram_c, gram_out, out_sem.at[1])
    finish.start()
    sent_a()
    sent_b()
    store.wait()
    finish.wait()


def power_step(sketch, band_tiles, far_tiles, far_owner, far_local, far_count):
    any_space = pl.BlockSpec(memory_space=pl.ANY)
    scalars = pl.BlockSpec(memory_space=pltpu.SMEM)
    dma = pltpu.SemaphoreType.DMA
    return pl.pallas_call(
        range_kernel,
        out_shape=(
            jax.ShapeDtypeStruct((BLOCKS, B, B), F32),
            jax.ShapeDtypeStruct((B, B), F32),
        ),
        in_specs=[any_space, any_space, any_space, scalars, scalars, scalars],
        out_specs=(any_space, any_space),
        scratch_shapes=[
            pltpu.VMEM((N_PANEL + 3, B, B), BF16),
            pltpu.VMEM((N_PANEL + 3, B, B), BF16),
            pltpu.VMEM((BLOCKS, 3, B, B), BF16),
            pltpu.VMEM((BLOCKS, SLOTS, B, B), BF16),
            pltpu.VMEM((BLOCKS, B, B), F32),
            pltpu.VMEM((B, B), F32),
            pltpu.VMEM((B, B), F32),
            pltpu.VMEM((N_ROW, PART, B), F32),
            pltpu.VMEM((N_GRP, PART, B), F32),
            dma((3,)),
            dma((2, BLOCKS, N_ROW)),
            dma((2, BLOCKS)),
            dma((2, 2)),
            dma((2, 2)),
            dma((N_ROW,)),
            dma((N_ROW,)),
            dma((N_GRP,)),
            dma((N_GRP,)),
            dma((N_ROW,)),
            dma((N_ROW,)),
            dma((2,)),
        ],
        compiler_params=pltpu.CompilerParams(
            collective_id=0, has_side_effects=True, vmem_limit_bytes=56 * 1024 * 1024
        ),
        cost_estimate=pl.CostEstimate(
            flops=4 * 88 * B**3, bytes_accessed=15 << 20, transcendentals=0
        ),
    )(sketch, band_tiles, far_tiles, far_owner, far_local, far_count)


def body(sketch, band_tiles, far_tiles, far_owner, far_local, far_count):
    second, gram = power_step(sketch, band_tiles, far_tiles, far_owner, far_local, far_count)
    flat_rows = second.reshape(BLOCKS * B, B)
    lower_factor = jnp.linalg.cholesky(gram)
    solved = jax.scipy.linalg.solve_triangular(lower_factor, flat_rows.T, lower=True)
    scale_rows = math.sqrt(BLOCKS * B * N_ROW * N_GRP)
    basis = (solved.T * scale_rows).reshape(BLOCKS, B, B)
    factor = lower_factor.T / scale_rows
    return (basis, factor)


def solution(mesh):
    in_specs = (
        P(("row", "grp"), None, None),
        P(("row", "grp"), None, None, None),
        P(("row", "grp"), None, None, None),
        P(("row", "grp"), None),
        P(("row", "grp"), None),
        P(("row", "grp")),
    )
    out_specs = (P(("row", "grp"), None, None), P())
    return jax.shard_map(body, mesh=mesh, in_specs=in_specs, out_specs=out_specs, check_vma=False)
```

time: 755 us -> 281 us (0.37)
  waiting for transfers between devices: 530 us -> 0 us
  Pallas kernels: 0 us -> 211 us
  local copies, waits for them, and re-layouts: 63.9 us -> 7.66 us
  matrix products: 42.2 us -> 4.43 us
  starting transfers between devices: 31.8 us -> 0 us
  blocking collectives: 14.6 us -> 0 us
  between operations: 15.7 us -> 2.03 us
    all_to_all x2 -> x0, waiting for transfers between devices: 381 us -> none  [fetch_blocks(): lax.all_to_all(tile_stack, 'row', split_axis=0, concat_axis=0, tiled=True)]
    pallas_call x0 -> x1, Pallas kernels: none -> 211 us  [power_step(): pl.pallas_call(range_kernel, out_shape=(jax.ShapeDtypeStruct((BLOCKS, B,...]
    psum x1 -> x0, waiting for transfers between devices: 148 us -> none  [body(): gram = lax.psum(gram_part, ('row', 'grp'))]
    dot_general x9 -> x0, matrix products: 38.6 us -> none  [the longest x2 18.2 us: apply_matrix(): jnp.einsum('isab,isbk->iak', far_tiles, remote, preferred_element_type=jn...]
    gather x4 -> x0, local copies, waits for them, and re-layouts: 34.7 us -> none  [the longest x2 20.2 us: fetch_blocks(): return arrived.reshape(row_count * capacity, width, columns_k)[slot_index]]
    all_to_all x3 -> x0, local copies, waits for them, and re-layouts: 16.8 us -> none  [the longest x1 16.7 us: fetch_blocks(): lax.all_to_all(tile_stack, 'row', split_axis=0, concat_axis=0, tiled=True)]
    ppermute x4 -> x0, starting transfers between devices: 16.2 us -> none  [the longest x2 12.2 us: with_halo(): lax.ppermute(tail, axis, [(i, (i + 1) % count) for i in range(ends)])]
    all_to_all x2 -> x0, starting transfers between devices: 15.5 us -> none  [fetch_blocks(): lax.all_to_all(tile_stack, 'row', split_axis=0, concat_axis=0, tiled=True)]
  transfers between devices with their start and end apart: 7 -> 0, of which waited for: 3 -> 0; matrix products, arithmetic and copies ran while one was open for 9% -> 0% of each run, Pallas kernels for 0% -> 0%
where the time goes in v1:
time: 281 us
  Pallas kernels  211 us (75%)
  other arithmetic  55.2 us (20%)
  local copies, waits for them, and re-layouts  7.66 us (3%)
  matrix products  4.43 us (2%)
    pallas_call x1, Pallas kernels, power_step(): pl.pallas_call(range_kernel, out_shape=(jax.ShapeDtypeStruct((BLOCKS, B,...  211 us
    another operation x6, other arithmetic, body(): lower_factor = jnp.linalg.cholesky(gram)  34 us
    another operation x2, other arithmetic, body(): jax.scipy.linalg.solve_triangular(lower_factor, flat_rows.T, lower=True)  19.9 us

profile of v1, /device:TPU:1, one launch (start us, length us, event | category | flops | bytes accessed | tf_op | source)
XLA Modules:
  0.0 280.7 jit_solution(11954522460956803545)
XLA Ops:
  0.6 0.1 triangular_solve.57
  0.7 211.4 %shard_map.77 = (f32[8,256,256]{2,1,0:T(8,128)}, f32[256,256]{1,0:T(8,128)}) custom-call(bf16[8,256,256]{2,1,0:T(8,128)(2,1)} %sketch.1, bf16[8,3,256,256]{3,2,1,0:T(8,128)(2,1)} %band.1, bf16[8,8,256,256]{3,2,1,0:T(8,128)(2,1)} %far.1, s32[8,8]{1,0:T(8,128)} %owner.1, s32[8,8]{1,0:T(8,128)} %local.1, s32[8]{0:T(128)} %count.1), custom_call_target="tpu_custom_call" | custom-call | flops 5905580032 | bytes 15728640 | tf_op jit(solution)/shard_map/pallas_call | solution.py:340
  212.1 1.1 copy.8
  213.2 0.0 copy-start
  213.2 1.1 fusion.3
  214.3 11.7 %cholesky.50 = f32[128,128]{1,0:T(8,128)S(1)} custom-call(f32[128,128]{1,0:T(8,128)S(1)} %cholesky.118), custom_call_target="Cholesky" | custom-call | tf_op jit(solution)/shard_map/jit(cholesky)/cholesky | solution.py:383
  226.1 9.8 %custom-call.15 = f32[1,128,128]{1,2,0:T(8,128)S(1)} custom-call(f32[1,128,128]{2,1,0:T(8,128)S(1)} %get-tuple-element.31), custom_call_target="InvertDiagBlocksLowerTriangular" | custom-call | tf_op jit(solution)/shard_map/jit(cholesky)/cholesky | solution.py:383
  235.9 0.2 constant_dynamic-update-slice_fusion.1
  236.1 0.3 convolution_subtract_fusion.1
  236.4 11.7 %cholesky.105 = f32[128,128]{1,0:T(8,128)S(1)} custom-call(f32[128,128]{1,0:T(8,128)S(1)} %convolution_subtract_fusion.1), custom_call_target="Cholesky" | custom-call | tf_op jit(solution)/shard_map/jit(cholesky)/cholesky | solution.py:383
  248.1 0.7 compare_reduce_fusion
  250.1 0.8 copy.10
  250.9 3.9 %while.1 = (s32[]{:T(128)}, f32[256,256]{1,0:T(8,128)S(1)}, s32[2,2]{1,0:T(2,128)S(1)}, f32[2,128,128]{2,1,0:T(8,128)S(1)}, s32[]{:T(128)}) while((s32[]{:T(128)}, f32[256,256]{1,0:T(8,128)S(1)}, s32[2,2]{1,0:T(2,128)S(1)}, f32[2,128,128]{2,1,0:T(8,128)S(1)}, s32[]{:T(128)}) %tuple.29), condition=%wide.while_cond, body=%wide.while_body.sunk | while | flops 2 | bytes 131189 | solution.py:384
  251.0 0.6 fusion.16
  251.5 1.3 bitcast_dynamic-update-slice_fusion.2
  252.9 0.6 fusion.16
  253.5 1.3 bitcast_dynamic-update-slice_fusion.2
  254.8 19.9 %custom-call.16 = f32[2,128,128]{1,2,0:T(8,128)S(1)} custom-call(f32[2,128,128]{2,1,0:T(8,128)S(1)} %get-tuple-element.13), custom_call_target="InvertDiagBlocksLowerTriangular" | custom-call | tf_op jit(solution)/shard_map/jit(_solve_triangular)/triangular_solve | solution.py:384
  274.7 0.0 copy-done
  274.7 1.1 fusion.1
  275.8 1.8 convolution_subtract_fusion
  277.6 1.1 fusion.6
  278.7 0.2 fusion
  278.9 1.8 copy.11
  (9 shorter events, 0.2 us)
Async XLA Ops:
  213.2 61.6 %copy-start = (f32[8,256,256]{2,1,0:T(8,128)S(1)}, f32[8,256,256]{2,1,0:T(8,128)}, u32[]{:S(2)}) copy-start(f32[8,256,256]{2,1,0:T(8,128)} %get-tuple-element.5) | copy-start | bytes 6291460

commit v2 on v1

--- a/solution.py
+++ b/solution.py
@@ -20,6 +20,8 @@
 PART = B // N_ROW
 F32 = jnp.float32
 BF16 = jnp.bfloat16
+SUB, LANE = 8, 128
+SCALE = math.sqrt(BLOCKS * B * N_ROW * N_GRP)
 
 
 def dot(a, b):
@@ -331,6 +333,110 @@
     sent_b()
     store.wait()
     finish.wait()
+
+
+def factor_kernel(gram, second, basis, factor, m, inv_v, second_v, out_v, sem):
+    load = pltpu.make_async_copy(second, second_v, sem.at[0])
+    load.start()
+    tile = (SUB, LANE)
+    halves = range(B // LANE)
+    lanes = lax.broadcasted_iota(jnp.int32, tile, 1)
+    subs = lax.broadcasted_iota(jnp.int32, tile, 0)
+    m[...] = gram[...]
+
+    def row_of(a, r):
+        return jnp.broadcast_to(a[r : r + 1, :], tile)
+
+    def column_of(a, c):
+        return jnp.broadcast_to(a[:, c : c + 1], tile)
+
+    def at(i, l):
+        return (pl.ds(i * SUB, SUB), pl.ds(l * LANE, LANE))
+
+    for g in range(B // SUB):
+        home, first = g * SUB // LANE, g * SUB % LANE
+        inside = (lanes >= first) & (lanes < first + SUB)
+        pivot = [m[at(g, l)] for l in halves]
+        columns = [column_of(pivot[home], first + c) for c in range(SUB)]
+        s = {(r, c): row_of(columns[c], r) for c in range(SUB) for r in range(c, SUB)}
+        roots, ratios = [], {}
+        for j in range(SUB):
+            d = s[j, j]
+            inverse = 1.0 / d
+            roots.append(lax.rsqrt(d))
+            old = {r: s[max(r, j), min(r, j)] for r in range(SUB) if r != j}
+            new = {r: old[r] * inverse for r in old}
+            for r in old:
+                for c in old:
+                    if c <= r:
+                        s[r, c] = s[r, c] - old[r] * new[c]
+            for r in old:
+                s[max(r, j), min(r, j)] = new[r]
+                if r > j:
+                    ratios[r, j] = new[r]
+            s[j, j] = -inverse
+        unit = jnp.where(inside, (lanes - first == subs).astype(F32), pivot[home])
+        source = [unit if l == home else pivot[l] for l in halves]
+        rows = [[row_of(source[l], r) for l in halves] for r in range(SUB)]
+        weights = []
+        for c in range(SUB):
+            per = []
+            for l in halves:
+                terms = [s[max(r, c), min(r, c)] * rows[r][l] for r in range(SUB)]
+                while len(terms) > 1:
+                    terms = [terms[k] + terms[k + 1] for k in range(0, len(terms), 2)]
+                per.append(terms[0])
+            weights.append(per)
+        for i in range(g + 1, B // SUB):
+            left = m[at(i, home)]
+            columns = [column_of(left, first + c) for c in range(SUB)]
+            for l in halves:
+                value = jnp.where(inside, 0.0, left) if l == home else m[at(i, l)]
+                terms = [columns[c] * weights[c][l] for c in range(SUB)]
+                while len(terms) > 1:
+                    terms = [terms[k] + terms[k + 1] for k in range(0, len(terms), 2)]
+                m[at(i, l)] = value + terms[0]
+        upper = [row_of(pivot[home], r) for r in range(SUB)]
+        inv_tiles = [jnp.zeros(tile, F32) for _ in halves]
+        fac_tiles = [jnp.zeros(tile, F32) for _ in halves]
+        for r in range(SUB):
+            for j in range(r):
+                upper[r] = upper[r] - ratios[r, j] * upper[j]
+                for l in halves:
+                    rows[r][l] = rows[r][l] - ratios[r, j] * rows[j][l]
+            here = subs == r
+            for l in halves:
+                if l <= home:
+                    inv_tiles[l] = jnp.where(here, rows[r][l] * roots[r], inv_tiles[l])
+                if l > home:
+                    fac_tiles[l] = jnp.where(here, rows[r][l] * roots[r], fac_tiles[l])
+                if l == home:
+                    fac_tiles[l] = jnp.where(here, upper[r] * roots[r], fac_tiles[l])
+        inv_tiles[home] = jnp.where(lanes < first + SUB, inv_tiles[home], 0.0)
+        fac_tiles[home] = jnp.where(lanes - first >= subs, fac_tiles[home], 0.0)
+        for l in halves:
+            inv_v[at(g, l)] = inv_tiles[l] * SCALE
+            factor[at(g, l)] = fac_tiles[l] * (1.0 / SCALE)
+
+    turned = inv_v[...].T
+    top = turned.astype(BF16)
+    rest = (turned - top.astype(F32)).astype(BF16)
+    load.wait()
+
+    def store(i):
+        return pltpu.make_async_copy(out_v.at[i], basis.at[i], sem.at[1 + i])
+
+    @pl.loop(0, BLOCKS)
+    def _(i):
+        x = second_v[i]
+        x_top = x.astype(BF16)
+        x_rest = (x - x_top.astype(F32)).astype(BF16)
+        out_v[i] = dot(x_top, top) + (dot(x_top, rest) + dot(x_rest, top))
+        store(i).start()
+
+    @pl.loop(0, BLOCKS)
+    def _(i):
+        store(i).wait()
 
 
 def power_step(sketch, band_tiles, far_tiles, far_owner, far_local, far_count):
@@ -377,15 +483,31 @@
     )(sketch, band_tiles, far_tiles, far_owner, far_local, far_count)
 
 
+def orthonormalize(gram, second):
+    whole = pl.BlockSpec(memory_space=pltpu.VMEM)
+    any_space = pl.BlockSpec(memory_space=pl.ANY)
+    return pl.pallas_call(
+        factor_kernel,
+        out_shape=(
+            jax.ShapeDtypeStruct((BLOCKS, B, B), F32),
+            jax.ShapeDtypeStruct((B, B), F32),
+        ),
+        in_specs=[whole, any_space],
+        out_specs=(any_space, whole),
+        scratch_shapes=[
+            pltpu.VMEM((B, B), F32),
+            pltpu.VMEM((B, B), F32),
+            pltpu.VMEM((BLOCKS, B, B), F32),
+            pltpu.VMEM((BLOCKS, B, B), F32),
+            pltpu.SemaphoreType.DMA((1 + BLOCKS,)),
+        ],
+        compiler_params=pltpu.CompilerParams(vmem_limit_bytes=32 * 1024 * 1024),
+    )(gram, second)
+
+
 def body(sketch, band_tiles, far_tiles, far_owner, far_local, far_count):
     second, gram = power_step(sketch, band_tiles, far_tiles, far_owner, far_local, far_count)
-    flat_rows = second.reshape(BLOCKS * B, B)
-    lower_factor = jnp.linalg.cholesky(gram)
-    solved = jax.scipy.linalg.solve_triangular(lower_factor, flat_rows.T, lower=True)
-    scale_rows = math.sqrt(BLOCKS * B * N_ROW * N_GRP)
-    basis = (solved.T * scale_rows).reshape(BLOCKS, B, B)
-    factor = lower_factor.T / scale_rows
-    return (basis, factor)
+    return orthonormalize(gram, second)
 
 
 def solution(mesh):

time: 281 us -> 230 us (0.82)
  other arithmetic: 55.2 us -> 0 us
  Pallas kernels: 211 us -> 227 us
  local copies, waits for them, and re-layouts: 7.66 us -> 2.53 us
  matrix products: 4.43 us -> 0 us
    another operation x8 -> x0, other arithmetic: 53.9 us -> none  [the longest x6 34 us: body(): lower_factor = jnp.linalg.cholesky(gram)]
    pallas_call x0 -> x1, Pallas kernels: none -> 15.1 us  [orthonormalize(): pl.pallas_call(factor_kernel, out_shape=(jax.ShapeDtypeStruct((BLOCKS, B,...]
    another operation x5 -> x0, matrix products: 4.43 us -> none  [the longest x3 3.96 us: body(): jax.scipy.linalg.solve_triangular(lower_factor, flat_rows.T, lower=True)]
    another operation x9 -> x0, local copies, waits for them, and re-layouts: 3.92 us -> none
where the time goes in v2:
time: 230 us
  Pallas kernels  227 us (99%)
  local copies, waits for them, and re-layouts  2.53 us (1%)
    pallas_call x1, Pallas kernels, power_step(): pl.pallas_call(range_kernel, out_shape=(jax.ShapeDtypeStruct((BLOCKS, B,...  211 us
    pallas_call x1, Pallas kernels, orthonormalize(): pl.pallas_call(factor_kernel, out_shape=(jax.ShapeDtypeStruct((BLOCKS, B,...  15.1 us

profile of v2, /device:TPU:1, one launch (start us, length us, event | category | flops | bytes accessed | tf_op | source)
XLA Modules:
  0.0 229.9 jit_solution(5972728804865163563)
XLA Ops:
  0.6 211.4 %shard_map.77 = (f32[8,256,256]{2,1,0:T(8,128)}, f32[256,256]{1,0:T(8,128)}) custom-call(bf16[8,256,256]{2,1,0:T(8,128)(2,1)} %sketch.1, bf16[8,3,256,256]{3,2,1,0:T(8,128)(2,1)} %band.1, bf16[8,8,256,256]{3,2,1,0:T(8,128)(2,1)} %far.1, s32[8,8]{1,0:T(8,128)} %owner.1, s32[8,8]{1,0:T(8,128)} %local.1, s32[8]{0:T(128)} %count.1), custom_call_target="tpu_custom_call" | custom-call | flops 5905580032 | bytes 15728640 | tf_op jit(solution)/shard_map/pallas_call | solution.py:446
  212.0 0.0 copy-start
  212.0 1.6 copy-done
  213.6 0.0 copy-start.1
  213.6 0.9 copy-done.1
  214.6 15.1 %shard_map.78 = (f32[8,256,256]{2,1,0:T(8,128)}, f32[256,256]{1,0:T(8,128)}) custom-call(f32[256,256]{1,0:T(8,128)S(1)} %copy-done.1, f32[8,256,256]{2,1,0:T(8,128)S(1)} %copy-done), custom_call_target="tpu_custom_call" | custom-call | tf_op jit(solution)/shard_map/pallas_call | solution.py:489
Async XLA Ops:
  212.0 1.6 copy-start
  213.6 0.9 copy-start.1

commit v3 on v2

--- a/solution.py
+++ b/solution.py
@@ -1,4 +1,3 @@
-import functools
 import math
 
 import jax
@@ -18,6 +17,10 @@
 N_PANEL = N_ROW * BLOCKS
 ZERO, LEFT, RIGHT = N_PANEL, N_PANEL + 1, N_PANEL + 2
 PART = B // N_ROW
+CAP = 6
+QUARTERS = 4
+UNITS = 8
+TALL, WIDE = B // 4, B // 2
 F32 = jnp.float32
 BF16 = jnp.bfloat16
 SUB, LANE = 8, 128
@@ -31,8 +34,9 @@
 def range_kernel(
     sketch, band, far, owner, local, count,
     second_out, gram_out,
-    panel_a, panel_b, band_v, far_v, acc, gram_v, gram_c, parts, shares,
-    load_sem, recv_sem, send_sem, halo_send, halo_recv,
+    panel_a, panel_b, band_v, far_v, acc, packed, gram_v, gram_c, parts, shares,
+    wants_v, wants_in, index_v, wants_s, index_s,
+    load_sem, recv_sem, send_sem, halo_send, halo_recv, wants_send, wants_recv, table_sem,
     scatter_send, scatter_recv, share_send, share_recv, spread_send, spread_recv, out_sem,
 ):
     row, grp = lax.axis_index("row"), lax.axis_index("grp")
@@ -43,10 +47,18 @@
     before_id = (before // N_GRP, before % N_GRP)
     own = row * BLOCKS
 
-    load_panel = pltpu.make_async_copy(sketch, panel_a.at[pl.ds(own, BLOCKS)], load_sem.at[0])
-    load_band = pltpu.make_async_copy(band, band_v, load_sem.at[1])
-    load_far = pltpu.make_async_copy(far, far_v, load_sem.at[2])
-    load_panel.start()
+    def load_unit(n):
+        h, q = n // QUARTERS, n % QUARTERS
+        return pltpu.make_async_copy(
+            sketch.at[:, pl.ds(q * TALL, TALL), pl.ds(h * WIDE, WIDE)],
+            panel_a.at[n, pl.ds(own, BLOCKS)],
+            load_sem.at[2 + n],
+        )
+
+    load_band = pltpu.make_async_copy(band, band_v, load_sem.at[0])
+    load_far = pltpu.make_async_copy(far, far_v, load_sem.at[1])
+    for n in range(UNITS):
+        load_unit(n).start()
     load_band.start()
     load_far.start()
 
@@ -65,112 +77,228 @@
 
     greet(after_id)
     greet(before_id)
+
+    table = (8, 128)
+    lanes = lax.broadcasted_iota(jnp.int32, table, 1)
+    subs = lax.broadcasted_iota(jnp.int32, table, 0)
+    nothing = jnp.zeros(table, jnp.int32)
+
+    def spread_entry(e, carry):
+        owners, locals_, counts = carry
+        i, s = e // SLOTS, e % SLOTS
+        here = lanes == e
+        return (
+            jnp.where(here, owner[i, s], owners),
+            jnp.where(here, local[i, s], locals_),
+            jnp.where(here, count[i], counts),
+        )
+
+    owners, locals_, counts = lax.fori_loop(
+        0, BLOCKS * SLOTS, spread_entry, (nothing, nothing, nothing)
+    )
+
+    def rank_entry(e, carry):
+        wants, seen, ranks = carry
+        i, s = e // SLOTS, e % SLOTS
+        name = owner[i, s]
+        hit = (lanes // SLOTS) == name
+        wants = jnp.where(hit & (seen == lanes % SLOTS), local[i, s], wants)
+        seen = seen + hit.astype(jnp.int32)
+        ranks = ranks + ((owners == name) & (lanes > e)).astype(jnp.int32)
+        return wants, seen, ranks
+
+    wants, _, ranks = lax.fori_loop(
+        0, BLOCKS * SLOTS, rank_entry, (nothing, nothing, nothing)
+    )
+    wants_v[...] = wants
+    from_x = (x - owners // SIDE + SIDE) % SIDE
+    from_z = (z - owners % SIDE + SIDE) % SIDE
+    index = nothing
+    for q in range(QUARTERS):
+        away = from_z if q % 2 == 0 else from_x
+        if q // 2 == 1:
+            away = (SIDE - away) % SIDE
+        leaf = away // 2
+        at = owners * BLOCKS + locals_ + leaf * (ranks - locals_)
+        at = jnp.where(lanes % SLOTS < counts, at, ZERO)
+        index = jnp.where(subs == q, at, index)
+    index_v[...] = index
+    index_copy = pltpu.make_async_copy(index_v, index_s, table_sem.at[0])
+    index_copy.start()
+
     for panel in (panel_a, panel_b):
-        panel[ZERO] = jnp.zeros((B, B), BF16)
-    load_panel.wait()
+        panel[:, ZERO] = jnp.zeros((UNITS, TALL, WIDE), BF16)
+    for n in range(UNITS):
+        load_unit(n).wait()
     pl.semaphore_wait(barrier, N_ROW - 1 + N_GRP - 1 + 2)
 
+    around = (
+        ((x + 1) % SIDE * SIDE + z, 1),
+        ((x + SIDE - 1) % SIDE * SIDE + z, 0),
+        (x * SIDE + (z + 1) % SIDE, 3),
+        (x * SIDE + (z + SIDE - 1) % SIDE, 2),
+    )
+    tell = [
+        pltpu.make_async_remote_copy(
+            src_ref=wants_v,
+            dst_ref=wants_in.at[side],
+            send_sem=wants_send.at[side],
+            recv_sem=wants_recv.at[side],
+            device_id=(neighbour, grp),
+            device_id_type=MESH,
+        )
+        for neighbour, side in around
+    ]
+    for one in tell:
+        one.start()
+
     def gather_steps(app, panel):
-        def place(b, first, second):
-            swap = b % 2
-            sign = 1 - 2 * ((b // 2) % 2)
+        def turn(n):
+            return n % 2, 1 - 2 * ((n // 2) % 2)
+
+        def place(n, first, second):
+            swap, sign = turn(n)
             to_x = (x + 2 * SIDE + sign * (first * (1 - swap) + second * swap)) % SIDE
             to_z = (z + 2 * SIDE + sign * (first * swap + second * (1 - swap))) % SIDE
             return to_x * SIDE + to_z
 
-        def send(b, u, v, first, second):
-            slot = place(b, -u, -v) * BLOCKS + b
+        def send(n, u, v, first, second):
+            slots = pl.ds(place(n, -u, -v) * BLOCKS, BLOCKS)
             to_u, to_v = (u + first) % SIDE, (v + second) % SIDE
             pltpu.make_async_remote_copy(
-                src_ref=panel.at[slot],
-                dst_ref=panel.at[slot],
-                send_sem=send_sem.at[app, b],
-                recv_sem=recv_sem.at[app, b, to_u * SIDE + to_v],
-                device_id=(place(b, first, second), grp),
+                src_ref=panel.at[n, slots],
+                dst_ref=panel.at[n, slots],
+                send_sem=send_sem.at[app, n],
+                recv_sem=recv_sem.at[app, n, to_u * SIDE + to_v],
+                device_id=(place(n, first, second), grp),
                 device_id_type=MESH,
             ).start()
 
-        def arrived(b, u, v):
-            slot = place(b, -u, -v) * BLOCKS + b
+        def send_leaf(n, u, v, second):
+            swap, sign = turn(n)
+            side = 2 * (1 - swap) + (1 - second * sign) // 2
+            source = place(n, -u, -v)
+            to_v = (v + second) % SIDE
+            leaf = u * 2 + to_v - 2
+            blocks = [panel[n, source * BLOCKS + b] for b in range(BLOCKS)]
+            for k in range(CAP):
+                wanted = wants_s[side, 0, source * SLOTS + k]
+                out = blocks[0]
+                for b in range(1, BLOCKS):
+                    out = jnp.where(wanted == b, blocks[b], out)
+                packed[n, leaf, k] = out
+            pltpu.make_async_remote_copy(
+                src_ref=packed.at[n, leaf],
+                dst_ref=panel.at[n, pl.ds(source * BLOCKS, CAP)],
+                send_sem=send_sem.at[app, n],
+                recv_sem=recv_sem.at[app, n, u * SIDE + to_v],
+                device_id=(place(n, 0, second), grp),
+                device_id_type=MESH,
+            ).start()
+
+        def arrived(n, u, v):
+            slots = pl.ds(place(n, -u, -v) * BLOCKS, CAP if v >= 2 else BLOCKS)
             pltpu.make_async_copy(
-                panel.at[slot], panel.at[slot], recv_sem.at[app, b, u * SIDE + v]
+                panel.at[n, slots], panel.at[n, slots], recv_sem.at[app, n, u * SIDE + v]
             ).wait()
 
-        def send_own(b):
-            send(b, 0, 0, 1, 0)
-            send(b, 0, 0, -1, 0)
-            send(b, 0, 0, 0, 1)
-            send(b, 0, 0, 0, -1)
+        def send_own(n):
+            send(n, 0, 0, 1, 0)
+            send(n, 0, 0, -1, 0)
+            send(n, 0, 0, 0, 1)
 
         def forward():
-            @pl.loop(0, BLOCKS)
-            def _(b):
-                arrived(b, 1, 0)
-                send(b, 1, 0, 1, 0)
-                send(b, 1, 0, 0, 1)
-                send(b, 1, 0, 0, -1)
-                arrived(b, 3, 0)
-                send(b, 3, 0, 0, 1)
-                send(b, 3, 0, 0, -1)
-
-            @pl.loop(0, BLOCKS)
-            def _(b):
-                arrived(b, 2, 0)
-                send(b, 2, 0, 0, 1)
-                send(b, 2, 0, 0, -1)
-                arrived(b, 0, 1)
-                send(b, 0, 1, 0, 1)
-
-            @pl.loop(0, BLOCKS)
-            def _(b):
-                arrived(b, 1, 1)
-                send(b, 1, 1, 0, 1)
-                arrived(b, 3, 1)
-                send(b, 3, 1, 0, 1)
-
-            @pl.loop(0, BLOCKS)
-            def _(b):
-                arrived(b, 2, 1)
-                send(b, 2, 1, 0, 1)
-
-            @pl.loop(0, BLOCKS)
-            def _(b):
+            @pl.loop(0, UNITS)
+            def _(n):
+                send_leaf(n, 0, 0, -1)
+
+            @pl.loop(0, UNITS)
+            def _(n):
+                arrived(n, 1, 0)
+                send(n, 1, 0, 1, 0)
+                send(n, 1, 0, 0, 1)
+                send_leaf(n, 1, 0, -1)
+                arrived(n, 3, 0)
+                send(n, 3, 0, 0, 1)
+                send_leaf(n, 3, 0, -1)
+
+            @pl.loop(0, UNITS)
+            def _(n):
+                arrived(n, 2, 0)
+                send(n, 2, 0, 0, 1)
+                send_leaf(n, 2, 0, -1)
+                arrived(n, 0, 1)
+                send_leaf(n, 0, 1, 1)
+
+            @pl.loop(0, UNITS)
+            def _(n):
+                arrived(n, 1, 1)
+                send_leaf(n, 1, 1, 1)
+                arrived(n, 3, 1)
+                send_leaf(n, 3, 1, 1)
+
+            @pl.loop(0, UNITS)
+            def _(n):
+                arrived(n, 2, 1)
+                send_leaf(n, 2, 1, 1)
+
+            @pl.loop(0, UNITS)
+            def _(n):
                 for u in range(SIDE):
-                    arrived(b, u, 3)
+                    arrived(n, u, 3)
                 for u in range(SIDE):
-                    arrived(b, u, 2)
+                    arrived(n, u, 2)
+
+        def clear():
+            @pl.loop(0, UNITS)
+            def _(n):
+                for u in range(SIDE):
+                    for v in (2, 3):
+                        for k in range(CAP, BLOCKS):
+                            panel[n, place(n, -u, -v) * BLOCKS + k] = jnp.zeros((TALL, WIDE), BF16)
 
         def sent():
-            @pl.loop(0, BLOCKS)
-            def _(b):
+            total = 7 * BLOCKS + 8 * CAP
+
+            @pl.loop(0, UNITS)
+            def _(n):
                 pltpu.make_async_copy(
-                    panel.at[pl.ds(0, N_ROW - 1)],
-                    panel.at[pl.ds(0, N_ROW - 1)],
-                    send_sem.at[app, b],
+                    panel.at[n, pl.ds(0, total)],
+                    panel.at[n, pl.ds(0, total)],
+                    send_sem.at[app, n],
                 ).wait()
 
-        return send_own, forward, sent
-
-    def halo(app, panel):
+        return send_own, forward, sent, clear
+
+    def halo(app, panel, h):
+        units = pl.ds(h * QUARTERS, QUARTERS)
         tail = pltpu.make_async_remote_copy(
-            src_ref=panel.at[own + BLOCKS - 1],
-            dst_ref=panel.at[LEFT],
-            send_sem=halo_send.at[app, 0],
-            recv_sem=halo_recv.at[app, 0],
+            src_ref=panel.at[units, own + BLOCKS - 1],
+            dst_ref=panel.at[units, LEFT],
+            send_sem=halo_send.at[app, 2 * h],
+            recv_sem=halo_recv.at[app, 2 * h],
             device_id=after_id,
             device_id_type=MESH,
         )
         head = pltpu.make_async_remote_copy(
-            src_ref=panel.at[own],
-            dst_ref=panel.at[RIGHT],
-            send_sem=halo_send.at[app, 1],
-            recv_sem=halo_recv.at[app, 1],
+            src_ref=panel.at[units, own],
+            dst_ref=panel.at[units, RIGHT],
+            send_sem=halo_send.at[app, 2 * h + 1],
+            recv_sem=halo_recv.at[app, 2 * h + 1],
             device_id=before_id,
             device_id_type=MESH,
         )
         return head, tail
 
-    def near(panel, i):
+    def column(panel, h, at):
+        return jnp.concatenate(
+            [panel[h * QUARTERS + q, at(q)] for q in range(QUARTERS)], axis=0
+        )
+
+    def block_of(panel, halves, at):
+        return jnp.concatenate([column(panel, h, at) for h in halves], axis=1)
+
+    def near(panel, i, halves):
         left = jnp.where(i == 0, jnp.where(device == 0, ZERO, LEFT), own + i - 1)
         right = jnp.where(
             i == BLOCKS - 1,
@@ -178,61 +306,64 @@
             own + i + 1,
         )
         return (
-            dot(band_v[i, 0], panel[left])
-            + dot(band_v[i, 1], panel[own + i])
-            + dot(band_v[i, 2], panel[right])
-        )
-
-    def long_range(panel, i):
-        total = acc[i]
-        live_slots = count[i]
+            dot(band_v[i, 0], block_of(panel, halves, lambda q: left))
+            + dot(band_v[i, 1], block_of(panel, halves, lambda q: own + i))
+            + dot(band_v[i, 2], block_of(panel, halves, lambda q: right))
+        )
+
+    def long_range(panel, i, halves, total):
         for s in range(SLOTS):
-            live = (s < live_slots).astype(jnp.int32)
-            index = (owner[i, s] * BLOCKS + local[i, s]) * live + ZERO * (1 - live)
-            total = total + dot(far_v[i, s], panel[index])
+            remote = block_of(panel, halves, lambda q: index_s[q, i * SLOTS + s])
+            total = total + dot(far_v[i, s], remote)
         return total
 
-    send_own, forward, sent_a = gather_steps(0, panel_a)
-    head, tail = halo(0, panel_a)
-    pl.loop(0, BLOCKS)(send_own)
-    head.start()
-    tail.start()
+    both = (0, 1)
+    send_own, forward, sent_a, clear = gather_steps(0, panel_a)
+    pl.loop(0, UNITS)(send_own)
+    edges = [copy for h in both for copy in halo(0, panel_a, h)]
+    for copy in edges:
+        copy.start()
+    clear()
+    for one in tell:
+        one.wait()
+    wants_copy = pltpu.make_async_copy(wants_in, wants_s, table_sem.at[1])
+    wants_copy.start()
+    wants_copy.wait()
+    index_copy.wait()
+    forward()
     load_band.wait()
-    head.wait()
-    tail.wait()
+    load_far.wait()
+    for copy in edges:
+        copy.wait()
+
+    send_own, forward, sent_b, clear = gather_steps(1, panel_b)
+    edges = []
+    for h in both:
+
+        @pl.loop(0, BLOCKS)
+        def _(i):
+            total = long_range(panel_a, i, (h,), near(panel_a, i, (h,)))
+            value = total.astype(BF16)
+            for q in range(QUARTERS):
+                panel_b[h * QUARTERS + q, own + i] = value[q * TALL : (q + 1) * TALL]
+
+        pl.loop(h * QUARTERS, (h + 1) * QUARTERS)(send_own)
+        edges += halo(1, panel_b, h)
+        for copy in edges[-2:]:
+            copy.start()
+
+    sent_a()
+    clear()
+    forward()
+    for copy in edges:
+        copy.wait()
+
+    gram_v[...] = jnp.zeros((B, B), F32)
+    gram_c[...] = jnp.zeros((B, B), F32)
 
     @pl.loop(0, BLOCKS)
     def _(i):
-        acc[i] = near(panel_a, i)
-
-    forward()
-    load_far.wait()
-
-    send_own, forward, sent_b = gather_steps(1, panel_b)
-    head, tail = halo(1, panel_b)
-
-    @pl.loop(0, BLOCKS)
-    def _(i):
-        panel_b[own + i] = long_range(panel_a, i).astype(BF16)
-        send_own(i)
-
-    head.start()
-    tail.start()
-    head.wait()
-    tail.wait()
-
-    @pl.loop(0, BLOCKS)
-    def _(i):
-        acc[i] = near(panel_b, i)
-
-    forward()
-
-    gram_v[...] = jnp.zeros((B, B), F32)
-    gram_c[...] = jnp.zeros((B, B), F32)
-
-    @pl.loop(0, BLOCKS)
-    def _(i):
-        block = long_range(panel_b, i)
+        block = long_range(panel_b, i, both, near(panel_b, i, both))
         acc[i] = block
         top = block.astype(BF16)
         rest = block - top.astype(F32)
@@ -329,7 +460,6 @@
 
     finish = pltpu.make_async_copy(gram_c, gram_out, out_sem.at[1])
     finish.start()
-    sent_a()
     sent_b()
     store.wait()
     finish.wait()
@@ -452,20 +582,29 @@
         in_specs=[any_space, any_space, any_space, scalars, scalars, scalars],
         out_specs=(any_space, any_space),
         scratch_shapes=[
-            pltpu.VMEM((N_PANEL + 3, B, B), BF16),
-            pltpu.VMEM((N_PANEL + 3, B, B), BF16),
+            pltpu.VMEM((UNITS, N_PANEL + 3, TALL, WIDE), BF16),
+            pltpu.VMEM((UNITS, N_PANEL + 3, TALL, WIDE), BF16),
             pltpu.VMEM((BLOCKS, 3, B, B), BF16),
             pltpu.VMEM((BLOCKS, SLOTS, B, B), BF16),
             pltpu.VMEM((BLOCKS, B, B), F32),
+            pltpu.VMEM((UNITS, 8, CAP, TALL, WIDE), BF16),
             pltpu.VMEM((B, B), F32),
             pltpu.VMEM((B, B), F32),
             pltpu.VMEM((N_ROW, PART, B), F32),
             pltpu.VMEM((N_GRP, PART, B), F32),
-            dma((3,)),
-            dma((2, BLOCKS, N_ROW)),
-            dma((2, BLOCKS)),
-            dma((2, 2)),
-            dma((2, 2)),
+            pltpu.VMEM((8, 128), jnp.int32),
+            pltpu.VMEM((4, 8, 128), jnp.int32),
+            pltpu.VMEM((8, 128), jnp.int32),
+            pltpu.SMEM((4, 8, 128), jnp.int32),
+            pltpu.SMEM((8, 128), jnp.int32),
+            dma((2 + UNITS,)),
+            dma((2, UNITS, N_ROW)),
+            dma((2, UNITS)),
+            dma((2, 4)),
+            dma((2, 4)),
+            dma((4,)),
+            dma((4,)),
+            dma((2,)),
             dma((N_ROW,)),
             dma((N_ROW,)),
             dma((N_GRP,)),
@@ -475,7 +614,7 @@
             dma((2,)),
         ],
         compiler_params=pltpu.CompilerParams(
-            collective_id=0, has_side_effects=True, vmem_limit_bytes=56 * 1024 * 1024
+            collective_id=0, has_side_effects=True, vmem_limit_bytes=58 * 1024 * 1024
         ),
         cost_estimate=pl.CostEstimate(
             flops=4 * 88 * B**3, bytes_accessed=15 << 20, transcendentals=0
@@ -501,7 +640,7 @@
             pltpu.VMEM((BLOCKS, B, B), F32),
             pltpu.SemaphoreType.DMA((1 + BLOCKS,)),
         ],
-        compiler_params=pltpu.CompilerParams(vmem_limit_bytes=32 * 1024 * 1024),
+        compiler_params=pltpu.CompilerParams(vmem_limit_bytes=58 * 1024 * 1024),
     )(gram, second)
 
 

time: 230 us -> 213 us (0.926)
  Pallas kernels: 227 us -> 212 us
  local copies, waits for them, and re-layouts: 2.53 us -> 0 us
    pallas_call x1, Pallas kernels: 211 us -> 194 us  [power_step(): pl.pallas_call(range_kernel, out_shape=(jax.ShapeDtypeStruct((BLOCKS, B,...]
    unnamed x4 -> x0, local copies, waits for them, and re-layouts: 2.53 us -> none
where the time goes in v3:
time: 213 us; the launch traced here: 212 us
  Pallas kernels  212 us (100%)
    pallas_call x1, Pallas kernels, power_step(): pl.pallas_call(range_kernel, out_shape=(jax.ShapeDtypeStruct((BLOCKS, B,...  194 us
    pallas_call x1, Pallas kernels, orthonormalize(): pl.pallas_call(factor_kernel, out_shape=(jax.ShapeDtypeStruct((BLOCKS, B,...  17.2 us

profile of v3, /device:TPU:1, one launch (start us, length us, event | category | flops | bytes accessed | tf_op | source)
XLA Modules:
  0.0 212.5 jit_solution(16155334576179038309)
XLA Ops:
  0.6 194.5 %shard_map.77 = (f32[8,256,256]{2,1,0:T(8,128)}, f32[256,256]{1,0:T(8,128)}) custom-call(bf16[8,256,256]{2,1,0:T(8,128)(2,1)} %sketch.1, bf16[8,3,256,256]{3,2,1,0:T(8,128)(2,1)} %band.1, bf16[8,8,256,256]{3,2,1,0:T(8,128)(2,1)} %far.1, s32[8,8]{1,0:T(8,128)} %owner.1, s32[8,8]{1,0:T(8,128)} %local.1, s32[8]{0:T(128)} %count.1), custom_call_target="tpu_custom_call" | custom-call | flops 5905580032 | bytes 15728640 | tf_op jit(solution)/shard_map/pallas_call | solution.py:576
  195.1 17.2 %shard_map.78 = (f32[8,256,256]{2,1,0:T(8,128)}, f32[256,256]{1,0:T(8,128)}) custom-call(f32[256,256]{1,0:T(8,128)} %get-tuple-element.4.gram, f32[8,256,256]{2,1,0:T(8,128)} %get-tuple-element.5.second), custom_call_target="tpu_custom_call" | custom-call | tf_op jit(solution)/shard_map/pallas_call | solution.py:628

commit v4 on v3

--- a/solution.py
+++ b/solution.py
@@ -34,7 +34,7 @@
 def range_kernel(
     sketch, band, far, owner, local, count,
     second_out, gram_out,
-    panel_a, panel_b, band_v, far_v, acc, packed, gram_v, gram_c, parts, shares,
+    panel_a, panel_b, band_v, far_v, acc, packed, gram_v, gram_c, parts, shares, pair,
     wants_v, wants_in, index_v, wants_s, index_s,
     load_sem, recv_sem, send_sem, halo_send, halo_recv, wants_send, wants_recv, table_sem,
     scatter_send, scatter_recv, share_send, share_recv, spread_send, spread_recv, out_sem,
@@ -46,6 +46,17 @@
     after_id = (after // N_GRP, after % N_GRP)
     before_id = (before // N_GRP, before % N_GRP)
     own = row * BLOCKS
+    y, core = grp // 2, grp % 2
+    around = (
+        ((x + 1) % SIDE * SIDE + z, 1),
+        ((x + SIDE - 1) % SIDE * SIDE + z, 0),
+        (x * SIDE + (z + 1) % SIDE, 3),
+        (x * SIDE + (z + SIDE - 1) % SIDE, 2),
+    )
+
+    def along(k):
+        return (y + k) % SIDE * 2 + core
+
 
     def load_unit(n):
         h, q = n // QUARTERS, n % QUARTERS
@@ -67,16 +78,12 @@
     def greet(device_id):
         pl.semaphore_signal(barrier, inc=1, device_id=device_id, device_id_type=MESH)
 
-    @pl.loop(1, N_ROW)
-    def _(k):
-        greet(((row + k) % N_ROW, grp))
-
-    @pl.loop(1, N_GRP)
-    def _(k):
-        greet((row, (grp + k) % N_GRP))
-
+    for neighbour, _ in around:
+        greet((neighbour, grp))
     greet(after_id)
     greet(before_id)
+    for k in range(1, SIDE):
+        greet((row, along(k)))
 
     table = (8, 128)
     lanes = lax.broadcasted_iota(jnp.int32, table, 1)
@@ -130,14 +137,8 @@
         panel[:, ZERO] = jnp.zeros((UNITS, TALL, WIDE), BF16)
     for n in range(UNITS):
         load_unit(n).wait()
-    pl.semaphore_wait(barrier, N_ROW - 1 + N_GRP - 1 + 2)
-
-    around = (
-        ((x + 1) % SIDE * SIDE + z, 1),
-        ((x + SIDE - 1) % SIDE * SIDE + z, 0),
-        (x * SIDE + (z + 1) % SIDE, 3),
-        (x * SIDE + (z + SIDE - 1) % SIDE, 2),
-    )
+    pl.semaphore_wait(barrier, len(around) + 2 + SIDE - 1)
+
     tell = [
         pltpu.make_async_remote_copy(
             src_ref=wants_v,
@@ -207,10 +208,12 @@
             send(n, 0, 0, -1, 0)
             send(n, 0, 0, 0, 1)
 
-        def forward():
+        def forward(meanwhile):
             @pl.loop(0, UNITS)
             def _(n):
                 send_leaf(n, 0, 0, -1)
+
+            meanwhile()
 
             @pl.loop(0, UNITS)
             def _(n):
@@ -330,11 +333,18 @@
     wants_copy.start()
     wants_copy.wait()
     index_copy.wait()
-    forward()
+
+    def band_part(panel, edges):
+        for copy in edges:
+            copy.wait()
+
+        @pl.loop(0, BLOCKS)
+        def _(i):
+            acc[i] = near(panel, i, both)
+
     load_band.wait()
+    forward(lambda: band_part(panel_a, edges))
     load_far.wait()
-    for copy in edges:
-        copy.wait()
 
     send_own, forward, sent_b, clear = gather_steps(1, panel_b)
     edges = []
@@ -342,7 +352,7 @@
 
         @pl.loop(0, BLOCKS)
         def _(i):
-            total = long_range(panel_a, i, (h,), near(panel_a, i, (h,)))
+            total = long_range(panel_a, i, (h,), acc[i, :, pl.ds(h * WIDE, WIDE)])
             value = total.astype(BF16)
             for q in range(QUARTERS):
                 panel_b[h * QUARTERS + q, own + i] = value[q * TALL : (q + 1) * TALL]
@@ -354,17 +364,12 @@
 
     sent_a()
     clear()
-    forward()
-    for copy in edges:
-        copy.wait()
+    forward(lambda: band_part(panel_b, edges))
 
     gram_v[...] = jnp.zeros((B, B), F32)
     gram_c[...] = jnp.zeros((B, B), F32)
 
-    @pl.loop(0, BLOCKS)
-    def _(i):
-        block = long_range(panel_b, i, both, near(panel_b, i, both))
-        acc[i] = block
+    def add_gram(block):
         top = block.astype(BF16)
         rest = block - top.astype(F32)
         middle = rest.astype(BF16)
@@ -373,6 +378,16 @@
         gram_v[...] += dot(top_t, top) + dot(middle.T, middle)
         gram_c[...] += dot(top_t, middle) + dot(top_t, low)
 
+    acc[0] = long_range(panel_b, 0, both, acc[0])
+
+    @pl.loop(1, BLOCKS)
+    def _(i):
+        done = acc[i - 1]
+        total = long_range(panel_b, i, both, acc[i])
+        add_gram(done)
+        acc[i] = total
+
+    add_gram(acc[BLOCKS - 1])
     store = pltpu.make_async_copy(acc, second_out, out_sem.at[0])
     store.start()
     cross = gram_c[...]
@@ -403,30 +418,35 @@
     total = parts[0]
     for k in range(1, N_ROW):
         total = total + parts[k]
-    shares[grp] = total
+    shares[y] = total
 
     def share(k):
         return pltpu.make_async_remote_copy(
-            src_ref=shares.at[grp],
-            dst_ref=shares.at[grp],
+            src_ref=shares.at[y],
+            dst_ref=shares.at[y],
             send_sem=share_send.at[k],
             recv_sem=share_recv.at[k],
-            device_id=(row, (grp + k) % N_GRP),
+            device_id=(row, along(k)),
             device_id_type=MESH,
         )
 
-    @pl.loop(1, N_GRP)
-    def _(k):
+    for k in range(1, SIDE):
         share(k).start()
-
-    @pl.loop(1, N_GRP)
-    def _(k):
-        origin = (grp + N_GRP - k) % N_GRP
+    for k in range(1, SIDE):
+        origin = (y + SIDE - k) % SIDE
         pltpu.make_async_copy(shares.at[origin], shares.at[origin], share_recv.at[k]).wait()
-
-    total = shares[0]
-    for k in range(1, N_GRP):
-        total = total + shares[k]
+    pair[0] = (shares[0] + shares[1]) + (shares[2] + shares[3])
+    swap = pltpu.make_async_remote_copy(
+        src_ref=pair.at[0],
+        dst_ref=pair.at[1],
+        send_sem=share_send.at[0],
+        recv_sem=share_recv.at[0],
+        device_id=(row, y * 2 + 1 - core),
+        device_id_type=MESH,
+    )
+    swap.start()
+    swap.wait()
+    total = pair[0] + pair[1]
     gram_c[pl.ds(row * PART, PART)] = total
 
     def spread(k):
@@ -454,8 +474,7 @@
         scatter(k).wait_send()
         spread(k).wait_send()
 
-    @pl.loop(1, N_GRP)
-    def _(k):
+    for k in range(1, SIDE):
         share(k).wait_send()
 
     finish = pltpu.make_async_copy(gram_c, gram_out, out_sem.at[1])
@@ -591,7 +610,8 @@
             pltpu.VMEM((B, B), F32),
             pltpu.VMEM((B, B), F32),
             pltpu.VMEM((N_ROW, PART, B), F32),
-            pltpu.VMEM((N_GRP, PART, B), F32),
+            pltpu.VMEM((SIDE, PART, B), F32),
+            pltpu.VMEM((2, PART, B), F32),
             pltpu.VMEM((8, 128), jnp.int32),
             pltpu.VMEM((4, 8, 128), jnp.int32),
             pltpu.VMEM((8, 128), jnp.int32),
@@ -607,8 +627,8 @@
             dma((2,)),
             dma((N_ROW,)),
             dma((N_ROW,)),
-            dma((N_GRP,)),
-            dma((N_GRP,)),
+            dma((SIDE,)),
+            dma((SIDE,)),
             dma((N_ROW,)),
             dma((N_ROW,)),
             dma((2,)),

time: 213 us -> 208 us (0.977)
  Pallas kernels: 212 us -> 207 us
    pallas_call x1, Pallas kernels: 194 us -> 190 us  [power_step(): pl.pallas_call(range_kernel, out_shape=(jax.ShapeDtypeStruct((BLOCKS, B,...]
where the time goes in v4:
time: 208 us
  Pallas kernels  207 us (100%)
    pallas_call x1, Pallas kernels, power_step(): pl.pallas_call(range_kernel, out_shape=(jax.ShapeDtypeStruct((BLOCKS, B,...  190 us
    pallas_call x1, Pallas kernels, orthonormalize(): pl.pallas_call(factor_kernel, out_shape=(jax.ShapeDtypeStruct((BLOCKS, B,...  17.2 us

profile of v4, /device:TPU:1, one launch (start us, length us, event | category | flops | bytes accessed | tf_op | source)
XLA Modules:
  0.0 208.2 jit_solution(9906993544153501762)
XLA Ops:
  0.6 190.2 %shard_map.77 = (f32[8,256,256]{2,1,0:T(8,128)}, f32[256,256]{1,0:T(8,128)}) custom-call(bf16[8,256,256]{2,1,0:T(8,128)(2,1)} %sketch.1, bf16[8,3,256,256]{3,2,1,0:T(8,128)(2,1)} %band.1, bf16[8,8,256,256]{3,2,1,0:T(8,128)(2,1)} %far.1, s32[8,8]{1,0:T(8,128)} %owner.1, s32[8,8]{1,0:T(8,128)} %local.1, s32[8]{0:T(128)} %count.1), custom_call_target="tpu_custom_call" | custom-call | flops 5905580032 | bytes 15728640 | tf_op jit(solution)/shard_map/pallas_call | solution.py:595
  190.8 17.2 %shard_map.78 = (f32[8,256,256]{2,1,0:T(8,128)}, f32[256,256]{1,0:T(8,128)}) custom-call(f32[256,256]{1,0:T(8,128)} %get-tuple-element.4.gram, f32[8,256,256]{2,1,0:T(8,128)} %get-tuple-element.5.second), custom_call_target="tpu_custom_call" | custom-call | tf_op jit(solution)/shard_map/pallas_call | solution.py:648

commit v5 on v4

--- a/solution.py
+++ b/solution.py
@@ -21,6 +21,14 @@
 QUARTERS = 4
 UNITS = 8
 TALL, WIDE = B // 4, B // 2
+TREE = (
+    (((0, 0), ((1, 0), (0, 1), (-1, 0), (0, -1))),),
+    (((1, 0), ((1, 0), (0, 1), (0, -1))), ((0, 1), ((0, 1), (-1, 0)))),
+    (((2, 0), ((0, -1), (0, 1))), ((0, 2), ((1, 0), (-1, 0)))),
+    (((2, 3), ((0, -1), (1, 0))),),
+)
+INNER = [node for level in TREE for node, _ in level]
+LEAVES = [(u, v) for u in range(SIDE) for v in range(SIDE) if (u, v) not in INNER]
 F32 = jnp.float32
 BF16 = jnp.bfloat16
 SUB, LANE = 8, 128
@@ -32,10 +40,10 @@
 
 
 def range_kernel(
-    sketch, band, far, owner, local, count,
+    sketch, band, far, owner_in, local_in, count_in,
     second_out, gram_out,
     panel_a, panel_b, band_v, far_v, acc, packed, gram_v, gram_c, parts, shares, pair,
-    wants_v, wants_in, index_v, wants_s, index_s,
+    wants_v, wants_in, index_v, wants_s, index_s, owner, local, count,
     load_sem, recv_sem, send_sem, halo_send, halo_recv, wants_send, wants_recv, table_sem,
     scatter_send, scatter_recv, share_send, share_recv, spread_send, spread_recv, out_sem,
 ):
@@ -66,13 +74,6 @@
             load_sem.at[2 + n],
         )
 
-    load_band = pltpu.make_async_copy(band, band_v, load_sem.at[0])
-    load_far = pltpu.make_async_copy(far, far_v, load_sem.at[1])
-    for n in range(UNITS):
-        load_unit(n).start()
-    load_band.start()
-    load_far.start()
-
     barrier = pltpu.get_barrier_semaphore()
 
     def greet(device_id):
@@ -85,73 +86,24 @@
     for k in range(1, SIDE):
         greet((row, along(k)))
 
-    table = (8, 128)
-    lanes = lax.broadcasted_iota(jnp.int32, table, 1)
-    subs = lax.broadcasted_iota(jnp.int32, table, 0)
-    nothing = jnp.zeros(table, jnp.int32)
-
-    def spread_entry(e, carry):
-        owners, locals_, counts = carry
-        i, s = e // SLOTS, e % SLOTS
-        here = lanes == e
-        return (
-            jnp.where(here, owner[i, s], owners),
-            jnp.where(here, local[i, s], locals_),
-            jnp.where(here, count[i], counts),
-        )
-
-    owners, locals_, counts = lax.fori_loop(
-        0, BLOCKS * SLOTS, spread_entry, (nothing, nothing, nothing)
-    )
-
-    def rank_entry(e, carry):
-        wants, seen, ranks = carry
-        i, s = e // SLOTS, e % SLOTS
-        name = owner[i, s]
-        hit = (lanes // SLOTS) == name
-        wants = jnp.where(hit & (seen == lanes % SLOTS), local[i, s], wants)
-        seen = seen + hit.astype(jnp.int32)
-        ranks = ranks + ((owners == name) & (lanes > e)).astype(jnp.int32)
-        return wants, seen, ranks
-
-    wants, _, ranks = lax.fori_loop(
-        0, BLOCKS * SLOTS, rank_entry, (nothing, nothing, nothing)
-    )
-    wants_v[...] = wants
-    from_x = (x - owners // SIDE + SIDE) % SIDE
-    from_z = (z - owners % SIDE + SIDE) % SIDE
-    index = nothing
-    for q in range(QUARTERS):
-        away = from_z if q % 2 == 0 else from_x
-        if q // 2 == 1:
-            away = (SIDE - away) % SIDE
-        leaf = away // 2
-        at = owners * BLOCKS + locals_ + leaf * (ranks - locals_)
-        at = jnp.where(lanes % SLOTS < counts, at, ZERO)
-        index = jnp.where(subs == q, at, index)
-    index_v[...] = index
-    index_copy = pltpu.make_async_copy(index_v, index_s, table_sem.at[0])
-    index_copy.start()
-
-    for panel in (panel_a, panel_b):
-        panel[:, ZERO] = jnp.zeros((UNITS, TALL, WIDE), BF16)
+    load_band = pltpu.make_async_copy(band, band_v, load_sem.at[0])
+    load_far = pltpu.make_async_copy(far, far_v, load_sem.at[1])
+    for n in range(UNITS):
+        load_unit(n).start()
+    load_scalars = [
+        pltpu.make_async_copy(source, target, load_sem.at[2 + UNITS + k])
+        for k, (source, target) in enumerate(
+            ((owner_in, owner), (local_in, local), (count_in, count))
+        )
+    ]
+    for one in load_scalars:
+        one.start()
+    load_band.start()
+    load_far.start()
+
     for n in range(UNITS):
         load_unit(n).wait()
     pl.semaphore_wait(barrier, len(around) + 2 + SIDE - 1)
-
-    tell = [
-        pltpu.make_async_remote_copy(
-            src_ref=wants_v,
-            dst_ref=wants_in.at[side],
-            send_sem=wants_send.at[side],
-            recv_sem=wants_recv.at[side],
-            device_id=(neighbour, grp),
-            device_id_type=MESH,
-        )
-        for neighbour, side in around
-    ]
-    for one in tell:
-        one.start()
 
     def gather_steps(app, panel):
         def turn(n):
@@ -175,12 +127,12 @@
                 device_id_type=MESH,
             ).start()
 
-        def send_leaf(n, u, v, second):
+        def send_leaf(n, u, v, first, second):
             swap, sign = turn(n)
-            side = 2 * (1 - swap) + (1 - second * sign) // 2
+            side = 2 * (swap if first else 1 - swap) + (1 - (first + second) * sign) // 2
             source = place(n, -u, -v)
-            to_v = (v + second) % SIDE
-            leaf = u * 2 + to_v - 2
+            to = ((u + first) % SIDE, (v + second) % SIDE)
+            leaf = LEAVES.index(to)
             blocks = [panel[n, source * BLOCKS + b] for b in range(BLOCKS)]
             for k in range(CAP):
                 wanted = wants_s[side, 0, source * SLOTS + k]
@@ -192,76 +144,55 @@
                 src_ref=packed.at[n, leaf],
                 dst_ref=panel.at[n, pl.ds(source * BLOCKS, CAP)],
                 send_sem=send_sem.at[app, n],
-                recv_sem=recv_sem.at[app, n, u * SIDE + to_v],
-                device_id=(place(n, 0, second), grp),
+                recv_sem=recv_sem.at[app, n, to[0] * SIDE + to[1]],
+                device_id=(place(n, first, second), grp),
                 device_id_type=MESH,
             ).start()
 
         def arrived(n, u, v):
-            slots = pl.ds(place(n, -u, -v) * BLOCKS, CAP if v >= 2 else BLOCKS)
+            slots = pl.ds(place(n, -u, -v) * BLOCKS, CAP if (u, v) in LEAVES else BLOCKS)
             pltpu.make_async_copy(
                 panel.at[n, slots], panel.at[n, slots], recv_sem.at[app, n, u * SIDE + v]
             ).wait()
 
+        def edges_of(n, node, steps, leaves):
+            for first, second in steps:
+                to = ((node[0] + first) % SIDE, (node[1] + second) % SIDE)
+                if (to in LEAVES) == leaves:
+                    (send_leaf if leaves else send)(n, *node, first, second)
+
         def send_own(n):
-            send(n, 0, 0, 1, 0)
-            send(n, 0, 0, -1, 0)
-            send(n, 0, 0, 0, 1)
+            edges_of(n, *TREE[0][0], False)
 
         def forward(meanwhile):
             @pl.loop(0, UNITS)
             def _(n):
-                send_leaf(n, 0, 0, -1)
+                edges_of(n, *TREE[0][0], True)
 
             meanwhile()
+            for level in TREE[1:]:
+
+                @pl.loop(0, UNITS)
+                def _(n):
+                    for node, steps in level:
+                        arrived(n, *node)
+                        edges_of(n, node, steps, False)
+                        edges_of(n, node, steps, True)
 
             @pl.loop(0, UNITS)
             def _(n):
-                arrived(n, 1, 0)
-                send(n, 1, 0, 1, 0)
-                send(n, 1, 0, 0, 1)
-                send_leaf(n, 1, 0, -1)
-                arrived(n, 3, 0)
-                send(n, 3, 0, 0, 1)
-                send_leaf(n, 3, 0, -1)
-
-            @pl.loop(0, UNITS)
-            def _(n):
-                arrived(n, 2, 0)
-                send(n, 2, 0, 0, 1)
-                send_leaf(n, 2, 0, -1)
-                arrived(n, 0, 1)
-                send_leaf(n, 0, 1, 1)
-
-            @pl.loop(0, UNITS)
-            def _(n):
-                arrived(n, 1, 1)
-                send_leaf(n, 1, 1, 1)
-                arrived(n, 3, 1)
-                send_leaf(n, 3, 1, 1)
-
-            @pl.loop(0, UNITS)
-            def _(n):
-                arrived(n, 2, 1)
-                send_leaf(n, 2, 1, 1)
-
-            @pl.loop(0, UNITS)
-            def _(n):
-                for u in range(SIDE):
-                    arrived(n, u, 3)
-                for u in range(SIDE):
-                    arrived(n, u, 2)
+                for node in LEAVES:
+                    arrived(n, *node)
 
         def clear():
             @pl.loop(0, UNITS)
             def _(n):
-                for u in range(SIDE):
-                    for v in (2, 3):
-                        for k in range(CAP, BLOCKS):
-                            panel[n, place(n, -u, -v) * BLOCKS + k] = jnp.zeros((TALL, WIDE), BF16)
+                for u, v in LEAVES:
+                    for k in range(CAP, BLOCKS):
+                        panel[n, place(n, -u, -v) * BLOCKS + k] = jnp.zeros((TALL, WIDE), BF16)
 
         def sent():
-            total = 7 * BLOCKS + 8 * CAP
+            total = (len(INNER) - 1) * BLOCKS + len(LEAVES) * CAP
 
             @pl.loop(0, UNITS)
             def _(n):
@@ -326,6 +257,74 @@
     edges = [copy for h in both for copy in halo(0, panel_a, h)]
     for copy in edges:
         copy.start()
+    for one in load_scalars:
+        one.wait()
+    table = (8, 128)
+    lanes = lax.broadcasted_iota(jnp.int32, table, 1)
+    subs = lax.broadcasted_iota(jnp.int32, table, 0)
+    nothing = jnp.zeros(table, jnp.int32)
+
+    def spread_entry(e, carry):
+        owners, locals_, counts = carry
+        i, s = e // SLOTS, e % SLOTS
+        here = lanes == e
+        return (
+            jnp.where(here, owner[i, s], owners),
+            jnp.where(here, local[i, s], locals_),
+            jnp.where(here, count[i], counts),
+        )
+
+    owners, locals_, counts = lax.fori_loop(
+        0, BLOCKS * SLOTS, spread_entry, (nothing, nothing, nothing)
+    )
+
+    def rank_entry(e, carry):
+        wants, seen, ranks = carry
+        i, s = e // SLOTS, e % SLOTS
+        name = owner[i, s]
+        hit = (lanes // SLOTS) == name
+        wants = jnp.where(hit & (seen == lanes % SLOTS), local[i, s], wants)
+        seen = seen + hit.astype(jnp.int32)
+        ranks = ranks + ((owners == name) & (lanes > e)).astype(jnp.int32)
+        return wants, seen, ranks
+
+    wants, _, ranks = lax.fori_loop(
+        0, BLOCKS * SLOTS, rank_entry, (nothing, nothing, nothing)
+    )
+    wants_v[...] = wants
+    from_x = (x - owners // SIDE + SIDE) % SIDE
+    from_z = (z - owners % SIDE + SIDE) % SIDE
+    index = nothing
+    for q in range(QUARTERS):
+        u, v = (from_x, from_z) if q % 2 == 0 else (from_z, from_x)
+        if q // 2 == 1:
+            u, v = (SIDE - u) % SIDE, (SIDE - v) % SIDE
+        leaf = nothing
+        for a, b in LEAVES:
+            leaf = leaf + (u * SIDE + v == a * SIDE + b).astype(jnp.int32)
+        at = owners * BLOCKS + locals_ + leaf * (ranks - locals_)
+        at = jnp.where(lanes % SLOTS < counts, at, ZERO)
+        index = jnp.where(subs == q, at, index)
+    index_v[...] = index
+    index_copy = pltpu.make_async_copy(index_v, index_s, table_sem.at[0])
+    index_copy.start()
+
+    tell = [
+        pltpu.make_async_remote_copy(
+            src_ref=wants_v,
+            dst_ref=wants_in.at[side],
+            send_sem=wants_send.at[side],
+            recv_sem=wants_recv.at[side],
+            device_id=(neighbour, grp),
+            device_id_type=MESH,
+        )
+        for neighbour, side in around
+    ]
+    for one in tell:
+        one.start()
+
+    for panel in (panel_a, panel_b):
+        panel[:, ZERO] = jnp.zeros((UNITS, TALL, WIDE), BF16)
     clear()
     for one in tell:
         one.wait()
@@ -590,7 +589,6 @@
 
 def power_step(sketch, band_tiles, far_tiles, far_owner, far_local, far_count):
     any_space = pl.BlockSpec(memory_space=pl.ANY)
-    scalars = pl.BlockSpec(memory_space=pltpu.SMEM)
     dma = pltpu.SemaphoreType.DMA
     return pl.pallas_call(
         range_kernel,
@@ -598,7 +596,7 @@
             jax.ShapeDtypeStruct((BLOCKS, B, B), F32),
             jax.ShapeDtypeStruct((B, B), F32),
         ),
-        in_specs=[any_space, any_space, any_space, scalars, scalars, scalars],
+        in_specs=[any_space] * 6,
         out_specs=(any_space, any_space),
         scratch_shapes=[
             pltpu.VMEM((UNITS, N_PANEL + 3, TALL, WIDE), BF16),
@@ -606,7 +604,7 @@
             pltpu.VMEM((BLOCKS, 3, B, B), BF16),
             pltpu.VMEM((BLOCKS, SLOTS, B, B), BF16),
             pltpu.VMEM((BLOCKS, B, B), F32),
-            pltpu.VMEM((UNITS, 8, CAP, TALL, WIDE), BF16),
+            pltpu.VMEM((UNITS, len(LEAVES), CAP, TALL, WIDE), BF16),
             pltpu.VMEM((B, B), F32),
             pltpu.VMEM((B, B), F32),
             pltpu.VMEM((N_ROW, PART, B), F32),
@@ -617,7 +615,10 @@
             pltpu.VMEM((8, 128), jnp.int32),
             pltpu.SMEM((4, 8, 128), jnp.int32),
             pltpu.SMEM((8, 128), jnp.int32),
-            dma((2 + UNITS,)),
+            pltpu.SMEM((BLOCKS, SLOTS), jnp.int32),
+            pltpu.SMEM((BLOCKS, SLOTS), jnp.int32),
+            pltpu.SMEM((BLOCKS,), jnp.int32),
+            dma((5 + UNITS,)),
             dma((2, UNITS, N_ROW)),
             dma((2, UNITS)),
             dma((2, 4)),

time: 208 us -> 205 us (0.986)
  Pallas kernels: 207 us -> 204 us
    pallas_call x1, Pallas kernels: 190 us -> 187 us  [power_step(): pl.pallas_call(range_kernel, out_shape=(jax.ShapeDtypeStruct((BLOCKS, B,...]
where the time goes in v5:
time: 205 us
  Pallas kernels  204 us (100%)
    pallas_call x1, Pallas kernels, power_step(): pl.pallas_call(range_kernel, out_shape=(jax.ShapeDtypeStruct((BLOCKS, B,...  187 us
    pallas_call x1, Pallas kernels, orthonormalize(): pl.pallas_call(factor_kernel, out_shape=(jax.ShapeDtypeStruct((BLOCKS, B,...  17.2 us

profile of v5, /device:TPU:1, one launch (start us, length us, event | category | flops | bytes accessed | tf_op | source)
XLA Modules:
  0.0 205.1 jit_solution(11760924184182384782)
XLA Ops:
  0.6 187.1 %shard_map.77 = (f32[8,256,256]{2,1,0:T(8,128)}, f32[256,256]{1,0:T(8,128)}) custom-call(bf16[8,256,256]{2,1,0:T(8,128)(2,1)} %sketch.1, bf16[8,3,256,256]{3,2,1,0:T(8,128)(2,1)} %band.1, bf16[8,8,256,256]{3,2,1,0:T(8,128)(2,1)} %far.1, s32[8,8]{1,0:T(8,128)} %owner_in.1, s32[8,8]{1,0:T(8,128)} %local_in.1, s32[8]{0:T(128)} %count_in.1), custom_call_target="tpu_custom_call" | custom-call | flops 5905580032 | bytes 15728640 | tf_op jit(solution)/shard_map/pallas_call | solution.py:593
  187.7 17.2 %shard_map.78 = (f32[8,256,256]{2,1,0:T(8,128)}, f32[256,256]{1,0:T(8,128)}) custom-call(f32[256,256]{1,0:T(8,128)} %get-tuple-element.4.gram, f32[8,256,256]{2,1,0:T(8,128)} %get-tuple-element.5.second), custom_call_target="tpu_custom_call" | custom-call | tf_op jit(solution)/shard_map/pallas_call | solution.py:649

commit v6 on v5

--- a/solution.py
+++ b/solution.py
@@ -42,7 +42,7 @@
 def range_kernel(
     sketch, band, far, owner_in, local_in, count_in,
     second_out, gram_out,
-    panel_a, panel_b, band_v, far_v, acc, packed, gram_v, gram_c, parts, shares, pair,
+    panel_a0, panel_a1, panel_b0, panel_b1, band_v, far_v, acc, packed, gram_v, gram_c, parts, shares, pair,
     wants_v, wants_in, index_v, wants_s, index_s, owner, local, count,
     load_sem, recv_sem, send_sem, halo_send, halo_recv, wants_send, wants_recv, table_sem,
     scatter_send, scatter_recv, share_send, share_recv, spread_send, spread_recv, out_sem,
@@ -54,6 +54,7 @@
     after_id = (after // N_GRP, after % N_GRP)
     before_id = (before // N_GRP, before % N_GRP)
     own = row * BLOCKS
+    panels_a, panels_b = (panel_a0, panel_a1), (panel_b0, panel_b1)
     y, core = grp // 2, grp % 2
     around = (
         ((x + 1) % SIDE * SIDE + z, 1),
@@ -70,7 +71,7 @@
         h, q = n // QUARTERS, n % QUARTERS
         return pltpu.make_async_copy(
             sketch.at[:, pl.ds(q * TALL, TALL), pl.ds(h * WIDE, WIDE)],
-            panel_a.at[n, pl.ds(own, BLOCKS)],
+            panels_a[h].at[q, pl.ds(own, BLOCKS)],
             load_sem.at[2 + n],
         )
 
@@ -105,7 +106,9 @@
         load_unit(n).wait()
     pl.semaphore_wait(barrier, len(around) + 2 + SIDE - 1)
 
-    def gather_steps(app, panel):
+    def gather_steps(app, h, panel):
+        base = h * QUARTERS
+
         def turn(n):
             return n % 2, 1 - 2 * ((n // 2) % 2)
 
@@ -121,8 +124,8 @@
             pltpu.make_async_remote_copy(
                 src_ref=panel.at[n, slots],
                 dst_ref=panel.at[n, slots],
-                send_sem=send_sem.at[app, n],
-                recv_sem=recv_sem.at[app, n, to_u * SIDE + to_v],
+                send_sem=send_sem.at[app, base + n],
+                recv_sem=recv_sem.at[app, base + n, to_u * SIDE + to_v],
                 device_id=(place(n, first, second), grp),
                 device_id_type=MESH,
             ).start()
@@ -139,12 +142,12 @@
                 out = blocks[0]
                 for b in range(1, BLOCKS):
                     out = jnp.where(wanted == b, blocks[b], out)
-                packed[n, leaf, k] = out
+                packed[base + n, leaf, k] = out
             pltpu.make_async_remote_copy(
-                src_ref=packed.at[n, leaf],
+                src_ref=packed.at[base + n, leaf],
                 dst_ref=panel.at[n, pl.ds(source * BLOCKS, CAP)],
-                send_sem=send_sem.at[app, n],
-                recv_sem=recv_sem.at[app, n, to[0] * SIDE + to[1]],
+                send_sem=send_sem.at[app, base + n],
+                recv_sem=recv_sem.at[app, base + n, to[0] * SIDE + to[1]],
                 device_id=(place(n, first, second), grp),
                 device_id_type=MESH,
             ).start()
@@ -152,7 +155,7 @@
         def arrived(n, u, v):
             slots = pl.ds(place(n, -u, -v) * BLOCKS, CAP if (u, v) in LEAVES else BLOCKS)
             pltpu.make_async_copy(
-                panel.at[n, slots], panel.at[n, slots], recv_sem.at[app, n, u * SIDE + v]
+                panel.at[n, slots], panel.at[n, slots], recv_sem.at[app, base + n, u * SIDE + v]
             ).wait()
 
         def edges_of(n, node, steps, leaves):
@@ -161,51 +164,47 @@
                 if (to in LEAVES) == leaves:
                     (send_leaf if leaves else send)(n, *node, first, second)
 
+        def each(step):
+            return lambda: pl.loop(0, QUARTERS)(step)
+
+        def pass_on(depth):
+            def step(n):
+                for node, steps in TREE[depth]:
+                    if depth:
+                        arrived(n, *node)
+                        edges_of(n, node, steps, False)
+                    edges_of(n, node, steps, True)
+
+            pl.loop(0, QUARTERS)(step)
+
+        @each
         def send_own(n):
             edges_of(n, *TREE[0][0], False)
 
-        def forward(meanwhile):
-            @pl.loop(0, UNITS)
-            def _(n):
-                edges_of(n, *TREE[0][0], True)
-
-            meanwhile()
-            for level in TREE[1:]:
-
-                @pl.loop(0, UNITS)
-                def _(n):
-                    for node, steps in level:
-                        arrived(n, *node)
-                        edges_of(n, node, steps, False)
-                        edges_of(n, node, steps, True)
-
-            @pl.loop(0, UNITS)
-            def _(n):
-                for node in LEAVES:
-                    arrived(n, *node)
-
-        def clear():
-            @pl.loop(0, UNITS)
-            def _(n):
-                for u, v in LEAVES:
-                    for k in range(CAP, BLOCKS):
-                        panel[n, place(n, -u, -v) * BLOCKS + k] = jnp.zeros((TALL, WIDE), BF16)
-
-        def sent():
+        @each
+        def collect(n):
+            for node in LEAVES:
+                arrived(n, *node)
+
+        @each
+        def clear(n):
+            for u, v in LEAVES:
+                for k in range(CAP, BLOCKS):
+                    panel[n, place(n, -u, -v) * BLOCKS + k] = jnp.zeros((TALL, WIDE), BF16)
+
+        @each
+        def sent(n):
             total = (len(INNER) - 1) * BLOCKS + len(LEAVES) * CAP
-
-            @pl.loop(0, UNITS)
-            def _(n):
-                pltpu.make_async_copy(
-                    panel.at[n, pl.ds(0, total)],
-                    panel.at[n, pl.ds(0, total)],
-                    send_sem.at[app, n],
-                ).wait()
-
-        return send_own, forward, sent, clear
+            pltpu.make_async_copy(
+                panel.at[n, pl.ds(0, total)],
+                panel.at[n, pl.ds(0, total)],
+                send_sem.at[app, base + n],
+            ).wait()
+
+        return send_own, pass_on, collect, clear, sent
 
     def halo(app, panel, h):
-        units = pl.ds(h * QUARTERS, QUARTERS)
+        units = pl.ds(0, QUARTERS)
         tail = pltpu.make_async_remote_copy(
             src_ref=panel.at[units, own + BLOCKS - 1],
             dst_ref=panel.at[units, LEFT],
@@ -224,13 +223,11 @@
         )
         return head, tail
 
-    def column(panel, h, at):
-        return jnp.concatenate(
-            [panel[h * QUARTERS + q, at(q)] for q in range(QUARTERS)], axis=0
-        )
-
-    def block_of(panel, halves, at):
-        return jnp.concatenate([column(panel, h, at) for h in halves], axis=1)
+    def column(panel, at):
+        return jnp.concatenate([panel[q, at(q)] for q in range(QUARTERS)], axis=0)
+
+    def block_of(panels, halves, at):
+        return jnp.concatenate([column(panels[h], at) for h in halves], axis=1)
 
     def near(panel, i, halves):
         left = jnp.where(i == 0, jnp.where(device == 0, ZERO, LEFT), own + i - 1)
@@ -252,10 +249,21 @@
         return total
 
     both = (0, 1)
-    send_own, forward, sent_a, clear = gather_steps(0, panel_a)
-    pl.loop(0, UNITS)(send_own)
-    edges = [copy for h in both for copy in halo(0, panel_a, h)]
-    for copy in edges:
+    gathers = [
+        [gather_steps(app, h, panels[h]) for h in both]
+        for app, panels in enumerate((panels_a, panels_b))
+    ]
+    (own_a0, pass_a0, collect_a0, clear_a0, sent_a0), (
+        own_a1, pass_a1, collect_a1, clear_a1, sent_a1
+    ) = gathers[0]
+    (own_b0, pass_b0, collect_b0, clear_b0, sent_b0), (
+        own_b1, pass_b1, collect_b1, clear_b1, sent_b1
+    ) = gathers[1]
+
+    own_a0()
+    own_a1()
+    edges_a = [copy for h in both for copy in halo(0, panels_a[h], h)]
+    for copy in edges_a:
         copy.start()
     for one in load_scalars:
         one.wait()
@@ -323,9 +331,12 @@
     for one in tell:
         one.start()
 
-    for panel in (panel_a, panel_b):
-        panel[:, ZERO] = jnp.zeros((UNITS, TALL, WIDE), BF16)
-    clear()
+    for panel in panels_a + panels_b:
+        panel[:, ZERO] = jnp.zeros((QUARTERS, TALL, WIDE), BF16)
+    clear_a0()
+    clear_a1()
+    clear_b0()
+    clear_b1()
     for one in tell:
         one.wait()
     wants_copy = pltpu.make_async_copy(wants_in, wants_s, table_sem.at[1])
@@ -341,29 +352,50 @@
         def _(i):
             acc[i] = near(panel, i, both)
 
-    load_band.wait()
-    forward(lambda: band_part(panel_a, edges))
-    load_far.wait()
-
-    send_own, forward, sent_b, clear = gather_steps(1, panel_b)
-    edges = []
-    for h in both:
-
+    edges_b = []
+
+    def first_half(h, send_half):
         @pl.loop(0, BLOCKS)
         def _(i):
-            total = long_range(panel_a, i, (h,), acc[i, :, pl.ds(h * WIDE, WIDE)])
+            total = long_range(panels_a, i, (h,), acc[i, :, pl.ds(h * WIDE, WIDE)])
             value = total.astype(BF16)
             for q in range(QUARTERS):
-                panel_b[h * QUARTERS + q, own + i] = value[q * TALL : (q + 1) * TALL]
-
-        pl.loop(h * QUARTERS, (h + 1) * QUARTERS)(send_own)
-        edges += halo(1, panel_b, h)
-        for copy in edges[-2:]:
+                panels_b[h][q, own + i] = value[q * TALL : (q + 1) * TALL]
+
+        send_half()
+        copies = halo(1, panels_b[h], h)
+        for copy in copies:
             copy.start()
-
-    sent_a()
-    clear()
-    forward(lambda: band_part(panel_b, edges))
+        edges_b.extend(copies)
+
+    pass_a0(0)
+    pass_a1(0)
+    load_band.wait()
+    band_part(panels_a, edges_a)
+    pass_a0(1)
+    pass_a0(2)
+    pass_a1(1)
+    pass_a0(3)
+    pass_a1(2)
+    load_far.wait()
+    collect_a0()
+    first_half(0, own_b0)
+    pass_a1(3)
+    sent_a0()
+    pass_b0(0)
+    pass_b0(1)
+    collect_a1()
+    first_half(1, own_b1)
+    sent_a1()
+    pass_b1(0)
+    band_part(panels_b, edges_b)
+    pass_b0(2)
+    pass_b1(1)
+    pass_b0(3)
+    pass_b1(2)
+    pass_b1(3)
+    collect_b0()
+    collect_b1()
 
     gram_v[...] = jnp.zeros((B, B), F32)
     gram_c[...] = jnp.zeros((B, B), F32)
@@ -377,12 +409,12 @@
         gram_v[...] += dot(top_t, top) + dot(middle.T, middle)
         gram_c[...] += dot(top_t, middle) + dot(top_t, low)
 
-    acc[0] = long_range(panel_b, 0, both, acc[0])
+    acc[0] = long_range(panels_b, 0, both, acc[0])
 
     @pl.loop(1, BLOCKS)
     def _(i):
         done = acc[i - 1]
-        total = long_range(panel_b, i, both, acc[i])
+        total = long_range(panels_b, i, both, acc[i])
         add_gram(done)
         acc[i] = total
 
@@ -468,6 +500,9 @@
         theirs = pl.ds(((row + N_ROW - k) % N_ROW) * PART, PART)
         pltpu.make_async_copy(gram_c.at[theirs], gram_c.at[theirs], spread_recv.at[k]).wait()
 
+    finish = pltpu.make_async_copy(gram_c, gram_out, out_sem.at[1])
+    finish.start()
+
     @pl.loop(1, N_ROW)
     def _(k):
         scatter(k).wait_send()
@@ -476,9 +511,8 @@
     for k in range(1, SIDE):
         share(k).wait_send()
 
-    finish = pltpu.make_async_copy(gram_c, gram_out, out_sem.at[1])
-    finish.start()
-    sent_b()
+    sent_b0()
+    sent_b1()
     store.wait()
     finish.wait()
 
@@ -599,8 +633,10 @@
         in_specs=[any_space] * 6,
         out_specs=(any_space, any_space),
         scratch_shapes=[
-            pltpu.VMEM((UNITS, N_PANEL + 3, TALL, WIDE), BF16),
-            pltpu.VMEM((UNITS, N_PANEL + 3, TALL, WIDE), BF16),
+            pltpu.VMEM((QUARTERS, N_PANEL + 3, TALL, WIDE), BF16),
+            pltpu.VMEM((QUARTERS, N_PANEL + 3, TALL, WIDE), BF16),
+            pltpu.VMEM((QUARTERS, N_PANEL + 3, TALL, WIDE), BF16),
+            pltpu.VMEM((QUARTERS, N_PANEL + 3, TALL, WIDE), BF16),
             pltpu.VMEM((BLOCKS, 3, B, B), BF16),
             pltpu.VMEM((BLOCKS, SLOTS, B, B), BF16),
             pltpu.VMEM((BLOCKS, B, B), F32),

time: 205 us -> 199 us (0.971)
  Pallas kernels: 204 us -> 198 us
    pallas_call x1, Pallas kernels: 187 us -> 180 us  [power_step(): pl.pallas_call(range_kernel, out_shape=(jax.ShapeDtypeStruct((BLOCKS, B,...]
where the time goes in v6:
time: 199 us; the launch traced here: 198 us
  Pallas kernels  198 us (99%)
    pallas_call x1, Pallas kernels, power_step(): pl.pallas_call(range_kernel, out_shape=(jax.ShapeDtypeStruct((BLOCKS, B,...  180 us
    pallas_call x1, Pallas kernels, orthonormalize(): pl.pallas_call(factor_kernel, out_shape=(jax.ShapeDtypeStruct((BLOCKS, B,...  17.2 us

profile of v6, /device:TPU:1, one launch (start us, length us, event | category | flops | bytes accessed | tf_op | source)
XLA Modules:
  0.0 198.5 jit_solution(2086062656776699331)
XLA Ops:
  0.6 180.5 %shard_map.77 = (f32[8,256,256]{2,1,0:T(8,128)}, f32[256,256]{1,0:T(8,128)}) custom-call(bf16[8,256,256]{2,1,0:T(8,128)(2,1)} %sketch.1, bf16[8,3,256,256]{3,2,1,0:T(8,128)(2,1)} %band.1, bf16[8,8,256,256]{3,2,1,0:T(8,128)(2,1)} %far.1, s32[8,8]{1,0:T(8,128)} %owner_in.1, s32[8,8]{1,0:T(8,128)} %local_in.1, s32[8]{0:T(128)} %count_in.1), custom_call_target="tpu_custom_call" | custom-call | flops 5905580032 | bytes 15728640 | tf_op jit(solution)/shard_map/pallas_call | solution.py:627
  181.1 17.2 %shard_map.78 = (f32[8,256,256]{2,1,0:T(8,128)}, f32[256,256]{1,0:T(8,128)}) custom-call(f32[256,256]{1,0:T(8,128)} %get-tuple-element.4.gram, f32[8,256,256]{2,1,0:T(8,128)} %get-tuple-element.5.second), custom_call_target="tpu_custom_call" | custom-call | tf_op jit(solution)/shard_map/pallas_call | solution.py:685

commit v7 on v6

--- a/solution.py
+++ b/solution.py
@@ -16,7 +16,8 @@
 B = 256
 N_PANEL = N_ROW * BLOCKS
 ZERO, LEFT, RIGHT = N_PANEL, N_PANEL + 1, N_PANEL + 2
-PART = B // N_ROW
+TRI = 3 * B // 2
+PART = TRI // N_ROW
 CAP = 6
 QUARTERS = 4
 UNITS = 8
@@ -42,7 +43,7 @@
 def range_kernel(
     sketch, band, far, owner_in, local_in, count_in,
     second_out, gram_out,
-    panel_a0, panel_a1, panel_b0, panel_b1, band_v, far_v, acc, packed, gram_v, gram_c, parts, shares, pair,
+    panel_a0, panel_a1, panel_b0, panel_b1, band_v, far_v, acc, packed, gram_v, gram_c, corner, summed, parts, shares, pair,
     wants_v, wants_in, index_v, wants_s, index_s, owner, local, count,
     load_sem, recv_sem, send_sem, halo_send, halo_recv, wants_send, wants_recv, table_sem,
     scatter_send, scatter_recv, share_send, share_recv, spread_send, spread_recv, out_sem,
@@ -393,8 +394,17 @@
     pass_b1(1)
     pass_b0(3)
     pass_b1(2)
+    collect_b0()
+
+    def add_long_range(i, h):
+        columns = pl.ds(h * WIDE, WIDE)
+        acc[i, :, columns] = long_range(panels_b, i, (h,), acc[i, :, columns])
+
+    @pl.loop(0, BLOCKS)
+    def _(i):
+        add_long_range(i, 0)
+
     pass_b1(3)
-    collect_b0()
     collect_b1()
 
     gram_v[...] = jnp.zeros((B, B), F32)
@@ -409,25 +419,29 @@
         gram_v[...] += dot(top_t, top) + dot(middle.T, middle)
         gram_c[...] += dot(top_t, middle) + dot(top_t, low)
 
-    acc[0] = long_range(panels_b, 0, both, acc[0])
+    add_long_range(0, 1)
 
     @pl.loop(1, BLOCKS)
     def _(i):
         done = acc[i - 1]
-        total = long_range(panels_b, i, both, acc[i])
+        columns = pl.ds(WIDE, WIDE)
+        total = long_range(panels_b, i, (1,), acc[i, :, columns])
         add_gram(done)
-        acc[i] = total
+        acc[i, :, columns] = total
 
     add_gram(acc[BLOCKS - 1])
     store = pltpu.make_async_copy(acc, second_out, out_sem.at[0])
     store.start()
     cross = gram_c[...]
-    gram_v[...] += cross + cross.T
+    whole = gram_v[...] + cross + cross.T
+    corner[: B // 2] = whole[: B // 2, : B // 2]
+    corner[B // 2 : B] = whole[B // 2 :, : B // 2]
+    corner[B:] = whole[B // 2 :, B // 2 :]
 
     def scatter(k):
         to = (row + k) % N_ROW
         return pltpu.make_async_remote_copy(
-            src_ref=gram_v.at[pl.ds(to * PART, PART)],
+            src_ref=corner.at[pl.ds(to * PART, PART)],
             dst_ref=parts.at[row],
             send_sem=scatter_send.at[k],
             recv_sem=scatter_recv.at[k],
@@ -439,7 +453,7 @@
     def _(k):
         scatter(k).start()
 
-    parts[row] = gram_v[pl.ds(row * PART, PART)]
+    parts[row] = corner[pl.ds(row * PART, PART)]
 
     @pl.loop(1, N_ROW)
     def _(k):
@@ -478,13 +492,13 @@
     swap.start()
     swap.wait()
     total = pair[0] + pair[1]
-    gram_c[pl.ds(row * PART, PART)] = total
+    summed[pl.ds(row * PART, PART)] = total
 
     def spread(k):
         mine = pl.ds(row * PART, PART)
         return pltpu.make_async_remote_copy(
-            src_ref=gram_c.at[mine],
-            dst_ref=gram_c.at[mine],
+            src_ref=summed.at[mine],
+            dst_ref=summed.at[mine],
             send_sem=spread_send.at[k],
             recv_sem=spread_recv.at[k],
             device_id=((row + k) % N_ROW, grp),
@@ -498,9 +512,9 @@
     @pl.loop(1, N_ROW)
     def _(k):
         theirs = pl.ds(((row + N_ROW - k) % N_ROW) * PART, PART)
-        pltpu.make_async_copy(gram_c.at[theirs], gram_c.at[theirs], spread_recv.at[k]).wait()
-
-    finish = pltpu.make_async_copy(gram_c, gram_out, out_sem.at[1])
+        pltpu.make_async_copy(summed.at[theirs], summed.at[theirs], spread_recv.at[k]).wait()
+
+    finish = pltpu.make_async_copy(summed, gram_out, out_sem.at[1])
     finish.start()
 
     @pl.loop(1, N_ROW)
@@ -524,7 +538,10 @@
     halves = range(B // LANE)
     lanes = lax.broadcasted_iota(jnp.int32, tile, 1)
     subs = lax.broadcasted_iota(jnp.int32, tile, 0)
-    m[...] = gram[...]
+    m[: B // 2, : B // 2] = gram[: B // 2]
+    m[B // 2 :, : B // 2] = gram[B // 2 : B]
+    m[: B // 2, B // 2 :] = gram[B // 2 : B].T
+    m[B // 2 :, B // 2 :] = gram[B:]
 
     def row_of(a, r):
         return jnp.broadcast_to(a[r : r + 1, :], tile)
@@ -628,7 +645,7 @@
         range_kernel,
         out_shape=(
             jax.ShapeDtypeStruct((BLOCKS, B, B), F32),
-            jax.ShapeDtypeStruct((B, B), F32),
+            jax.ShapeDtypeStruct((TRI, B // 2), F32),
         ),
         in_specs=[any_space] * 6,
         out_specs=(any_space, any_space),
@@ -643,9 +660,11 @@
             pltpu.VMEM((UNITS, len(LEAVES), CAP, TALL, WIDE), BF16),
             pltpu.VMEM((B, B), F32),
             pltpu.VMEM((B, B), F32),
-            pltpu.VMEM((N_ROW, PART, B), F32),
-            pltpu.VMEM((SIDE, PART, B), F32),
-            pltpu.VMEM((2, PART, B), F32),
+            pltpu.VMEM((TRI, B // 2), F32),
+            pltpu.VMEM((TRI, B // 2), F32),
+            pltpu.VMEM((N_ROW, PART, B // 2), F32),
+            pltpu.VMEM((SIDE, PART, B // 2), F32),
+            pltpu.VMEM((2, PART, B // 2), F32),
             pltpu.VMEM((8, 128), jnp.int32),
             pltpu.VMEM((4, 8, 128), jnp.int32),
             pltpu.VMEM((8, 128), jnp.int32),

time: 199 us -> 197 us (0.990)
  Pallas kernels: 198 us -> 196 us
where the time goes in v7:
time: 197 us
  Pallas kernels  196 us (99%)
    pallas_call x1, Pallas kernels, power_step(): pl.pallas_call(range_kernel, out_shape=(jax.ShapeDtypeStruct((BLOCKS, B,...  179 us
    pallas_call x1, Pallas kernels, orthonormalize(): pl.pallas_call(factor_kernel, out_shape=(jax.ShapeDtypeStruct((BLOCKS, B,...  17.3 us

profile of v7, /device:TPU:1, one launch (start us, length us, event | category | flops | bytes accessed | tf_op | source)
XLA Modules:
  0.0 197.2 jit_solution(8519995201159145468)
XLA Ops:
  0.6 179.1 %shard_map.77 = (f32[8,256,256]{2,1,0:T(8,128)}, f32[384,128]{1,0:T(8,128)}) custom-call(bf16[8,256,256]{2,1,0:T(8,128)(2,1)} %sketch.1, bf16[8,3,256,256]{3,2,1,0:T(8,128)(2,1)} %band.1, bf16[8,8,256,256]{3,2,1,0:T(8,128)(2,1)} %far.1, s32[8,8]{1,0:T(8,128)} %owner_in.1, s32[8,8]{1,0:T(8,128)} %local_in.1, s32[8]{0:T(128)} %count_in.1), custom_call_target="tpu_custom_call" | custom-call | flops 5905580032 | bytes 15728640 | tf_op jit(solution)/shard_map/pallas_call | solution.py:644
  179.8 17.3 %shard_map.78 = (f32[8,256,256]{2,1,0:T(8,128)}, f32[256,256]{1,0:T(8,128)}) custom-call(f32[384,128]{1,0:T(8,128)} %get-tuple-element.4.gram, f32[8,256,256]{2,1,0:T(8,128)} %get-tuple-element.5.second), custom_call_target="tpu_custom_call" | custom-call | tf_op jit(solution)/shard_map/pallas_call | solution.py:704

commit v8 on v7

--- a/solution.py
+++ b/solution.py
@@ -625,8 +625,7 @@
     def store(i):
         return pltpu.make_async_copy(out_v.at[i], basis.at[i], sem.at[1 + i])
 
-    @pl.loop(0, BLOCKS)
-    def _(i):
+    for i in range(BLOCKS):
         x = second_v[i]
         x_top = x.astype(BF16)
         x_rest = (x - x_top.astype(F32)).astype(BF16)

time: 197 us -> 196 us (level)
  no operation moved by 1% of the time
where the time goes in v8:
time: 196 us
  Pallas kernels  195 us (99%)
    pallas_call x1, Pallas kernels, power_step(): pl.pallas_call(range_kernel, out_shape=(jax.ShapeDtypeStruct((BLOCKS, B,...  179 us
    pallas_call x1, Pallas kernels, orthonormalize(): pl.pallas_call(factor_kernel, out_shape=(jax.ShapeDtypeStruct((BLOCKS, B,...  16.2 us

profile of v8, /device:TPU:1, one launch (start us, length us, event | category | flops | bytes accessed | tf_op | source)
XLA Modules:
  0.0 196.2 jit_solution(10009359046262882501)
XLA Ops:
  0.6 179.1 %shard_map.77 = (f32[8,256,256]{2,1,0:T(8,128)}, f32[384,128]{1,0:T(8,128)}) custom-call(bf16[8,256,256]{2,1,0:T(8,128)(2,1)} %sketch.1, bf16[8,3,256,256]{3,2,1,0:T(8,128)(2,1)} %band.1, bf16[8,8,256,256]{3,2,1,0:T(8,128)(2,1)} %far.1, s32[8,8]{1,0:T(8,128)} %owner_in.1, s32[8,8]{1,0:T(8,128)} %local_in.1, s32[8]{0:T(128)} %count_in.1), custom_call_target="tpu_custom_call" | custom-call | flops 5905580032 | bytes 15728640 | tf_op jit(solution)/shard_map/pallas_call | solution.py:643
  179.8 16.2 %shard_map.78 = (f32[8,256,256]{2,1,0:T(8,128)}, f32[256,256]{1,0:T(8,128)}) custom-call(f32[384,128]{1,0:T(8,128)} %get-tuple-element.4.gram, f32[8,256,256]{2,1,0:T(8,128)} %get-tuple-element.5.second), custom_call_target="tpu_custom_call" | custom-call | tf_op jit(solution)/shard_map/pallas_call | solution.py:703
